TPU v7x, 256 devices: a whole 4x4x8 slice. The times are simulated.
256 devices in a mesh: wide: 32 (over y, z_hi, core), narrow: 8 (over x, z_lo).
Axes of the slice: x: 4, y: 4, z: 8 (z_hi: 4, z_lo: 2; z = z_hi * 2 + z_lo), core: 2. Of those that a mesh axis runs over, the one named last changes fastest.
Arguments:
- activations: bfloat16 [64, 48, 64, 512], P('wide', 'narrow'), may hold values from -6 to 6
- conv_weight: bfloat16 [3, 3, 3, 512, 16], replicated, may hold values from -0.0546875 to 0.0546875
- patch_weight: bfloat16 [64, 3072], replicated, may hold values from -0.75 to 0.75
- patch_bias: float32 [3072], replicated, may hold values from -3 to 3
- shift: float32 [3072], replicated, may hold values from -3 to 3
- scale: float32 [3072], replicated, may hold values from -0.9 to 0.9
- qkv_weight: bfloat16 [3072, 3, 2048], P('wide', None, 'narrow'), may hold values from -0.109375 to 0.109375
- qkv_bias: float32 [3, 2048], P(None, 'narrow'), may hold values from -3 to 3
- norm_gains: float32 [2, 128], replicated, may hold values from 0.25 to 1.75
Outputs:
- qkv: bfloat16 [3, 49152, 2048], P(None, 'wide', 'narrow')
All inputs are finite; a program needn't handle non-finite values.
Results may differ from a plain program's by a relative error of at most 0.0055.
Values may be sent and summed in bfloat16 or wider, within the bound.
A program may use at most 128 MiB of HBM per device.

v0:
```python
import jax
import jax.numpy as jnp
from jax import lax
from jax.sharding import PartitionSpec as P


def extended_2(x, sides, width):
    for axis, dim in sides:
        count, length = (lax.axis_size(axis), x.shape[dim])
        up = [(i, (i + 1) % count) for i in range(count - 1)]
        down = [(j, i) for i, j in up]
        last = lax.slice_in_dim(x, length - width, length, axis=dim)
        initial = lax.slice_in_dim(x, 0, width, axis=dim)
        before = lax.ppermute(last, axis, up)
        after = lax.ppermute(initial, axis, down)
        x = jnp.concatenate([before, x, after], axis=dim)
    return x


def shifted(x, axis, by):
    count = lax.axis_size(axis)
    pairs = [(i, i + by) for i in range(count) if 0 <= i + by < count]
    return lax.ppermute(x, axis, pairs)


def spatial_sums(products, row_count, col_count):
    result = []
    for time_tap in range(3):
        total = jnp.zeros(
            products.shape[:1] + (row_count, col_count, products.shape[-1]), jnp.float32
        )
        for row_tap in range(3):
            for col_tap in range(3):
                total = (
                    total
                    + products[
                        :,
                        row_tap : row_tap + row_count,
                        col_tap : col_tap + col_count,
                        time_tap,
                        row_tap,
                        col_tap,
                        :,
                    ]
                )
        result.append(total)
    return result


def embed(patches, patch_weight, patch_bias, shift, scale):
    embedded = jnp.dot(patches, patch_weight, preferred_element_type=jnp.float32) + patch_bias
    centre = embedded - jnp.mean(embedded, axis=-1, keepdims=True)
    spread = jnp.mean(centre * centre, axis=-1, keepdims=True)
    normed = centre * lax.rsqrt(spread + 1e-06)
    return (normed * (1.0 + scale) + shift).astype(jnp.bfloat16)


def head_norms(totals, qkv_bias, norm_gains, head_dim):
    token_count = totals.shape[0]
    biased = totals + qkv_bias.reshape(-1)
    split = biased.reshape(token_count, 3, -1, head_dim)

    def rms(values, gain):
        return values * lax.rsqrt(jnp.mean(values * values, axis=-1, keepdims=True) + 1e-06) * gain

    query = rms(split[:, 0], norm_gains[0])
    keys = rms(split[:, 1], norm_gains[1])
    stacked = jnp.stack([query, keys, split[:, 2]], axis=1)
    return stacked.reshape(token_count, 3, -1).astype(jnp.bfloat16)


def local(
    activations,
    conv_weight,
    patch_weight,
    patch_bias,
    shift,
    scale,
    qkv_weight,
    qkv_bias,
    norm_gains,
):
    frame_count, row_count, col_count, channels = activations.shape
    lat_channels = conv_weight.shape[4]
    head_dim = norm_gains.shape[1]
    conv_matrix = jnp.transpose(conv_weight, (3, 0, 1, 2, 4)).reshape(channels, 27 * lat_channels)
    acted = jax.nn.silu(activations.astype(jnp.float32)).astype(jnp.bfloat16)
    extended = extended_2(acted, (("narrow", 1),), 1)
    first_slab = lax.axis_index("wide") == 0
    earlier = shifted(extended, "wide", 1)
    own_copies = jnp.concatenate([extended[:1], extended[:1]], axis=0)
    earlier = jnp.where(first_slab, own_copies, earlier)
    frames_in = jnp.concatenate([earlier, extended], axis=0)
    padded = jnp.pad(frames_in, ((0, 0), (0, 0), (1, 1), (0, 0)))
    products = jnp.dot(
        padded.reshape(-1, channels), conv_matrix, preferred_element_type=jnp.float32
    )
    products = products.reshape(
        frames_in.shape[0], row_count + 2, col_count + 2, 3, 3, 3, lat_channels
    )
    tap_zero, tap_one, tap_two = spatial_sums(products, row_count, col_count)
    conv_sum = tap_two[2:] + tap_one[1:-1] + tap_zero[:-2]
    latents = conv_sum.astype(jnp.bfloat16)
    patches = latents.reshape(frame_count, row_count // 2, 2, col_count // 2, 2, lat_channels)
    patches = jnp.transpose(patches, (0, 1, 3, 2, 4, 5)).reshape(
        frame_count, row_count // 2, col_count // 2, 4 * lat_channels
    )
    features = embed(patches.reshape(-1, 4 * lat_channels), patch_weight, patch_bias, shift, scale)
    features = features.reshape(frame_count, row_count // 2, col_count // 2, -1)
    group = lax.all_gather(features, "narrow", axis=1, tiled=True)
    group = group.reshape(-1, patch_weight.shape[1])
    column_count = qkv_weight.shape[1] * qkv_weight.shape[2]
    piece = lax.all_gather(qkv_weight, "wide", axis=0, tiled=True)
    totals = jnp.dot(
        group, piece.reshape(piece.shape[0], column_count), preferred_element_type=jnp.float32
    )
    result = head_norms(totals, qkv_bias, norm_gains, head_dim)
    return jnp.transpose(result, (1, 0, 2))


def solution(mesh):
    placed = (
        P("wide", "narrow", None, None),
        P(),
        P(),
        P(),
        P(),
        P(),
        P("wide", None, "narrow"),
        P(None, "narrow"),
        P(),
    )
    return jax.shard_map(
        local, mesh=mesh, in_specs=placed, out_specs=P(None, "wide", "narrow"), check_vma=False
    )
```

profile of v0, /device:TPU:1, one launch (start us, length us, event | category | flops | bytes accessed | tf_op | source)
XLA Modules:
  0.0 299.4 jit_solution(149967265712087235)
XLA Ops:
  6.5 0.7 all-gather.5.cloned.1.call-update
  7.3 1.6 fusion.20
  8.9 4.4 %collective-permute-start = (bf16[2,1,64,512]{3,2,1,0:T(8,128)(2,1)S(1)}, bf16[2,1,64,512]{3,2,1,0:T(8,128)(2,1)S(1)}, u32[]{:S(2)}, u32[]{:S(2)}) collective-permute-start(bf16[2,1,64,512]{3,2,1,0:T(8,128)(2,1)S(1)} %get-tuple-element.30), channel_id=1, source_target_pairs={{0,1},{1,2},{2,3},{3,4},{4,5},{5,6},{6,7},{8,9},{9,10},{10,11},{11... | collective-permute-start | bytes 393224 | tf_op jit(solution)/shard_map/ppermute | solution.py:14
  13.3 1.3 collective-permute-start.1
  14.6 0.8 collective-permute-done
  15.5 4.2 %collective-permute-done.1 = bf16[2,1,64,512]{3,2,1,0:T(8,128)(2,1)S(1)} collective-permute-done((bf16[2,1,64,512]{3,2,1,0:T(8,128)(2,1)S(1)}, bf16[2,1,64,512]{3,2,1,0:T(8,128)(2,1)S(1)}, u32[]{:S(2)}, u32[]{:S(2)}) %collective-permute-start.1) | collective-permute-done | bytes 131104 | tf_op jit(solution)/shard_map/ppermute | solution.py:15
  19.6 0.7 copy-done.2
  20.3 0.1 pad_maximum_fusion
  20.4 6.5 %collective-permute-start.2 = (bf16[2,8,64,512]{3,2,1,0:T(8,128)(2,1)S(1)}, bf16[2,8,64,512]{3,2,1,0:T(8,128)(2,1)S(1)}, u32[]{:S(2)}, u32[]{:S(2)}) collective-permute-start(bf16[2,8,64,512]{3,2,1,0:T(8,128)(2,1)S(1)} %pad_maximum_fusion), channel_id=1, source_target_pairs={{0,8},{8,16},{16,24},{24,32},{32,40},{40,48},{48,56},{56,64},{64,7... | collective-permute-start | bytes 3145736 | tf_op jit(solution)/shard_map/ppermute | solution.py:23
  27.0 18.3 %collective-permute-done.2 = bf16[2,8,64,512]{3,2,1,0:T(8,128)(2,1)S(1)} collective-permute-done((bf16[2,8,64,512]{3,2,1,0:T(8,128)(2,1)S(1)}, bf16[2,8,64,512]{3,2,1,0:T(8,128)(2,1)S(1)}, u32[]{:S(2)}, u32[]{:S(2)}) %collective-permute-start.2) | collective-permute-done | bytes 1048608 | tf_op jit(solution)/shard_map/ppermute | solution.py:23
  45.2 0.1 maximum_select_fusion
  45.4 2.1 fusion.2
  47.5 0.3 fusion.30
  47.8 0.7 slice_add_fusion.4
  48.6 0.1 fusion.24
  48.7 0.1 copy.19
  48.9 0.2 copy.20
  49.2 0.4 copy-done.1
  49.5 0.6 fusion.32
  50.1 0.4 multiply_reduce_fusion
  50.6 1.5 add_convert_fusion
  52.2 33.6 %all-gather.5.cloned.1.call-done = bf16[3072,3,256]{2,0,1:T(8,128)(2,1)} async-done(((bf16[96,3,256]{2,0,1:T(8,128)(2,1)}), bf16[3072,3,256]{2,0,1:T(8,128)(2,1)}) %all-gather.5.cloned.1.call-update) | async-done | bytes 4718608 | tf_op jit(solution)/shard_map/all_gather | solution.py:113
  85.8 6.7 %copy.21 = bf16[3072,3,256]{0,2,1:T(8,128)(2,1)} copy(bf16[3072,3,256]{2,0,1:T(8,128)(2,1)} %all-gather.5.cloned.1.call-done) | data formatting | bytes 9437184 | tf_op jit(solution)/shard_map/all_gather | solution.py:113
  92.5 183.1 %all-gather.3.cloned.1.call-done = bf16[2,24,32,3072]{3,2,1,0:T(8,128)(2,1)} async-done(((bf16[2,3,32,3072]{3,2,1,0:T(8,128)(2,1)}), bf16[2,24,32,3072]{3,2,1,0:T(8,128)(2,1)}) %all-gather.3.cloned.1.call-update) | async-done | bytes 9437200 | tf_op jit(solution)/shard_map/all_gather | solution.py:110
  275.6 11.5 %convolution_add_fusion.1 = f32[1536,768]{0,1:T(8,128)S(1)} fusion(bf16[1536,3072]{1,0:T(8,128)(2,1)} %bitcast.49, bf16[3072,768]{0,1:T(8,128)(2,1)} %bitcast.44, f32[768]{0:T(1024)S(1)} %add.199), kind=kOutput, calls=%fused_computation.4 | convolution fusion | flops 7248936960 | bytes 18877440 | tf_op jit(solution)/shard_map/dot_general | solution.py:114
  287.1 0.4 multiply_reduce_fusion.2
  287.5 1.0 slice.294
  288.4 0.5 multiply_convert_fusion.1
  289.0 0.3 copy.27
  289.3 0.3 copy.28
  289.5 1.4 copy.29
  290.9 1.7 maximum_bitcast_fusion
  (28 shorter events, 0.3 us)
Async XLA Ops:
  6.5 38.8 %copy-start = (bf16[3,3,3,512,16]{3,4,2,1,0:T(8,128)(2,1)S(1)}, bf16[3,3,3,512,16]{3,4,2,1,0:T(8,128)(2,1)}, u32[]{:S(2)}) copy-start(bf16[3,3,3,512,16]{3,4,2,1,0:T(8,128)(2,1)} %param.10) | copy-start | bytes 1327108
  6.5 20.3 %copy-start.6 = (f32[3072]{0:T(1024)S(1)}, f32[3072]{0:T(1024)}, u32[]{:S(2)}) copy-start(f32[3072]{0:T(1024)} %param.14) | copy-start | bytes 36868
  6.5 79.3 %all-gather.5.cloned.1.call-start = ((), (), s32[]{:S(2)}) async-start(), calls=%async_computation.1 | async-start | bytes 4866048 | tf_op jit(solution)/shard_map/all_gather | solution.py:113
  7.3 268.3 %all-gather.3.cloned.1.call-start = ((), (), s32[]{:S(2)}) async-start(), calls=%async_computation | async-start | bytes 10616832 | tf_op jit(solution)/shard_map/all_gather | solution.py:110
  8.9 6.5 %collective-permute-start = (bf16[2,1,64,512]{3,2,1,0:T(8,128)(2,1)S(1)}, bf16[2,1,64,512]{3,2,1,0:T(8,128)(2,1)S(1)}, u32[]{:S(2)}, u32[]{:S(2)}) collective-permute-start(bf16[2,1,64,512]{3,2,1,0:T(8,128)(2,1)S(1)} %get-tuple-element.30), channel_id=1, source_target_pairs={{0,1},{1,2},{2,3},{3,4},{4,5},{5,6},{6,7},{8,9},{9,10},{10,11},{11... | collective-permute-start | bytes 393224 | tf_op jit(solution)/shard_map/ppermute | solution.py:14
  13.3 6.3 %collective-permute-start.1 = (bf16[2,1,64,512]{3,2,1,0:T(8,128)(2,1)S(1)}, bf16[2,1,64,512]{3,2,1,0:T(8,128)(2,1)S(1)}, u32[]{:S(2)}, u32[]{:S(2)}) collective-permute-start(bf16[2,1,64,512]{3,2,1,0:T(8,128)(2,1)S(1)} %get-tuple-element.31), channel_id=1, source_target_pairs={{1,0},{2,1},{3,2},{4,3},{5,4},{6,5},{7,6},{9,8},{10,9},{11,10},{12... | collective-permute-start | bytes 393224 | tf_op jit(solution)/shard_map/ppermute | solution.py:15
  19.6 0.7 copy-start.2
  20.4 24.8 %collective-permute-start.2 = (bf16[2,8,64,512]{3,2,1,0:T(8,128)(2,1)S(1)}, bf16[2,8,64,512]{3,2,1,0:T(8,128)(2,1)S(1)}, u32[]{:S(2)}, u32[]{:S(2)}) collective-permute-start(bf16[2,8,64,512]{3,2,1,0:T(8,128)(2,1)S(1)} %pad_maximum_fusion), channel_id=1, source_target_pairs={{0,8},{8,16},{16,24},{24,32},{32,40},{40,48},{48,56},{56,64},{64,7... | collective-permute-start | bytes 3145736 | tf_op jit(solution)/shard_map/ppermute | solution.py:23
  26.9 18.5 %copy-start.3 = (bf16[2,1,64,512]{3,2,1,0:T(8,128)(2,1)S(1)}, bf16[2,1,64,512]{3,2,1,0:T(8,128)(2,1)}, u32[]{:S(2)}) copy-start(bf16[2,1,64,512]{3,2,1,0:T(8,128)(2,1)} %copy-done.2) | copy-start | bytes 393220
  48.5 1.0 copy-start.1
  48.5 1.0 copy-start.4
  49.5 1.0 copy-start.5
  50.5 1.6 copy-start.7
  50.6 1.6 copy-start.8
Sparse Core Ops, SparseCore 0:
  9.9 75.8 all-gather.4
  87.6 187.9 all-gather.2
where the time goes:
time: 300 us; the launch traced here: 299 us
  waiting for transfers between devices  241 us (80%)
  matrix products  14.1 us (5%)
  between operations  13.6 us (5%)
  starting transfers between devices  12.2 us (4%)
  local copies, waits for them, and re-layouts  11.5 us (4%)
  other arithmetic  7.25 us (2%)
    all_gather x1, waiting for transfers between devices, local(): group = lax.all_gather(features, 'narrow', axis=1, tiled=True)  183 us
    all_gather x1, waiting for transfers between devices, local(): piece = lax.all_gather(qkv_weight, 'wide', axis=0, tiled=True)  33.6 us
    ppermute x1, waiting for transfers between devices, shifted(): return lax.ppermute(x, axis, pairs)  18.3 us
    dot_general x1, matrix products, local(): jnp.dot(group, piece.reshape(piece.shape[0], column_count), preferred_ele...  11.5 us
    all_gather x1, local copies, waits for them, and re-layouts, local(): piece = lax.all_gather(qkv_weight, 'wide', axis=0, tiled=True)  6.66 us
    ppermute x1, starting transfers between devices, shifted(): return lax.ppermute(x, axis, pairs)  6.47 us
  transfers between devices with their start and end apart: 5, of which 5 were waited for; matrix products, arithmetic and copies ran while one was open for 5% of the time, Pallas kernels for 0%

commit v1 on v0

v1 whole, which is shorter than its diff:
```python
import functools

import jax
import jax.numpy as jnp
from jax import lax
from jax.experimental import pallas as pl
from jax.experimental.pallas import tpu as pltpu
from jax.sharding import PartitionSpec as P

MESH = pl.DeviceIdType.MESH
F32 = jnp.float32
BF16 = jnp.bfloat16
CORES = 2
DEPTHS = 4
LANES = 128


def rolled(x, by):
    return pltpu.roll(x, by % x.shape[1], 1)


def halves(x):
    high = x.astype(BF16)
    return high, (x - high.astype(F32)).astype(BF16)


def dot(a, b):
    return lax.dot_general(a, b, (((1,), (0,)), ((), ())), preferred_element_type=F32)


def dot_t(a, b):
    return lax.dot_general(a, b, (((1,), (1,)), ((), ())), preferred_element_type=F32)


def front(
    sizes,
    act, cw, pw, pb, sh, sc, qw,
    x_out, r_out, m_out, e_out,
    act_v, cw_v, pw_v, pb_v, sh_v, sc_v, qw_v,
    part, got1, sum1, got2, own3, m_all, prod,
    a_v, b_v, at_v, ab_v, bm_v, bt_v, bb_v,
    wst, x_all, r_all,
    in_sem, act_sem, s1, g1, s2, g2, s3, g3, sx, gx, sr, gr, sh_sem, gh_sem,
):
    wides, narrows, rows, width = sizes
    span = qw.shape[1]
    w = lax.axis_index("wide")
    n = lax.axis_index("narrow")
    pairs = rows // 2
    group8 = wides // DEPTHS
    core = w % CORES
    depth = (w // CORES) % DEPTHS
    high = w // (CORES * DEPTHS)
    me8 = high * CORES + core

    def wide_of(q, z):
        return ((q // CORES) * DEPTHS + z) * CORES + q % CORES

    loads = []
    for k, (src, dst) in enumerate(
        [(pw, pw_v), (sc, sc_v), (sh, sh_v), (pb, pb_v), (qw, qw_v.at[:, pl.ds(0, span), :]), (cw, cw_v)]
    ):
        copy = pltpu.make_async_copy(src, dst, in_sem.at[k])
        copy.start()
        loads.append(copy)
    act_loads = []
    for k in range(pairs):
        for t in range(2):
            copy = pltpu.make_async_copy(
                act.at[t, pl.ds(2 * k, 2)], act_v.at[pl.ds(2 * k, 2), t], act_sem.at[2 * k + t]
            )
            copy.start()
            act_loads.append(copy)

    barrier = pltpu.get_barrier_semaphore()

    def greet(wide, narrow):
        pl.semaphore_signal(barrier, inc=1, device_id=(wide, narrow), device_id_type=MESH)

    for i in range(1, group8):
        greet(wide_of((me8 + i) % group8, depth), n)
    for i in range(1, DEPTHS):
        greet(wide_of(me8, (depth + i) % DEPTHS), n)
    for i in range(1, narrows):
        greet(w, (n + i) % narrows)
    has_next = w < wides - 1
    has_prev = w > 0
    for there, dw in ((has_next, 1), (has_prev, -1)):
        for dn in (-1, 0, 1):
            inside = there
            if dn == -1:
                inside = jnp.logical_and(there, n > 0)
            if dn == 1:
                inside = jnp.logical_and(there, n < narrows - 1)

            @pl.when(inside)
            def _():
                greet(w + dw, n + dn)

    sides = jnp.where(has_next, 1, 0) + jnp.where(has_prev, 1, 0)
    across = 1 + jnp.where(n > 0, 1, 0) + jnp.where(n < narrows - 1, 1, 0)
    expected = (group8 - 1) + (DEPTHS - 1) + (narrows - 1) + sides * across

    qw_v[:, span:, :] = jnp.zeros((3, qw_v.shape[1] - span, qw_v.shape[2]), BF16)
    for copy in loads[:5]:
        copy.wait()
    weight = pw_v[...].astype(F32)
    means = jnp.sum(weight, axis=1, keepdims=True) * (1.0 / width)
    bias_mean = jnp.sum(pb_v[...], axis=1, keepdims=True) * (1.0 / width)
    begin = w * span
    base = pl.multiple_of(jnp.minimum(begin // LANES, width // LANES - 2) * LANES, LANES)
    window = pl.ds(base, 2 * LANES)
    gain = 1.0 + sc_v[:, window]
    main = (pw_v[:, window].astype(F32) - means) * gain
    extra_b = (pb_v[:, window] - bias_mean) * gain
    extra_s = sh_v[:, window]
    pad = jnp.zeros((14, 2 * LANES), F32)
    stacked = jnp.concatenate([main, extra_b, extra_s, pad], axis=0)
    shift_by = (2 * LANES - (begin - base)) % (2 * LANES)
    stacked = pltpu.roll(stacked, shift_by, 1)[:, :LANES]
    lane = lax.broadcasted_iota(jnp.int32, stacked.shape, 1)
    stacked = jnp.where(lane < span, stacked, 0.0)
    top = stacked[:64]
    bottom = stacked[64:]
    row16 = lax.broadcasted_iota(jnp.int32, bottom.shape, 0)
    row_b = jnp.sum(jnp.where(row16 == 0, bottom, 0.0), axis=0, keepdims=True)
    row_s = jnp.sum(jnp.where(row16 == 1, bottom, 0.0), axis=0, keepdims=True)
    extras = jnp.zeros((8, qw.shape[2]), F32)
    for j in range(3):
        ext = jnp.where(row16 == 2 * j, row_b, jnp.where(row16 == 2 * j + 1, row_s, 0.0))
        hi, lo = halves(jnp.concatenate([top, ext], axis=0))
        res = dot(hi, qw_v[j]) + dot(lo, qw_v[j])
        part[:, :, j * 256 : (j + 1) * 256] = res[:64].reshape(8, 8, 256)
        extras = extras + res[64:72]
    for r in range(group8):
        part[r, :, 768:] = extras
    pl.semaphore_wait(barrier, expected)

    def sent(src, dst, ssem, gsem, to):
        return pltpu.make_async_remote_copy(
            src_ref=src, dst_ref=dst, send_sem=ssem, recv_sem=gsem, device_id=to, device_id_type=MESH
        )

    ring1 = []
    for i in range(1, group8):
        q = (me8 + i) % group8
        copy = sent(part.at[q], got1.at[i], s1.at[i], g1.at[i], (wide_of(q, depth), n))
        copy.start()
        ring1.append(copy)

    loads[5].wait()
    for k in range(pairs):
        act_loads[2 * k].wait()
        act_loads[2 * k + 1].wait()
        raw = act_v[2 * k : 2 * k + 2].reshape(256, act.shape[3]).astype(F32)
        acted = (raw / (1.0 + jnp.exp(-raw))).astype(BF16)
        res = dot_t(cw_v[...], acted)
        prod[2 * k] = res[:, :LANES]
        prod[2 * k + 1] = res[:, LANES:]

    full = (16 * (rows + 2), LANES)
    col = lax.broadcasted_iota(jnp.int32, full, 1) % 64
    early = lax.broadcasted_iota(jnp.int32, full, 1) < 64
    taps = []
    for a in range(3):
        moved = []
        for c in range(3):
            planes = []
            for h in range(-1, rows + 1):
                total = None
                for b in range(3):
                    src = h + b - 1
                    if 0 <= src < rows:
                        g = (a * 3 + b) * 3 + c
                        piece = prod[src, 16 * g : 16 * g + 16, :]
                        total = piece if total is None else total + piece
                planes.append(total)
            moved.append(jnp.concatenate(planes, axis=0))
        left = jnp.where(col == 0, 0.0, rolled(moved[0], 1))
        right = jnp.where(col == 63, 0.0, rolled(moved[2], -1))
        taps.append(moved[1] + left + right)
    swapped = rolled(taps[1], 64)
    here = taps[2] + jnp.where(early, 0.0, swapped)
    ahead = taps[0] + jnp.where(early, swapped, 0.0)
    copies = jnp.where(early, taps[1] + taps[0], rolled(taps[0], 64))
    here = here + jnp.where(w == 0, copies, 0.0)
    a_v[...] = here.reshape(rows + 2, 16, LANES)
    b_v[...] = ahead.reshape(rows + 2, 16, LANES)

    up = n > 0
    down = n < narrows - 1
    edges = [
        (b_v.at[pl.ds(1, rows)], bm_v, has_next, has_prev, (w + 1, n)),
        (a_v.at[0], ab_v, up, down, (w, n - 1)),
        (a_v.at[rows + 1], at_v, down, up, (w, n + 1)),
        (b_v.at[0], bb_v, jnp.logical_and(has_next, up), jnp.logical_and(has_prev, down), (w + 1, n - 1)),
        (b_v.at[rows + 1], bt_v, jnp.logical_and(has_next, down), jnp.logical_and(has_prev, up), (w + 1, n + 1)),
    ]
    edge_copies = []
    for k, (src, dst, gives, gets, to) in enumerate(edges):
        copy = sent(src, dst, sh_sem.at[k], gh_sem.at[k], to)
        edge_copies.append(copy)

        @pl.when(gives)
        def _():
            copy.start()

        @pl.when(jnp.logical_not(gets))
        def _():
            dst[...] = jnp.zeros(dst.shape, F32)

    hi, lo = halves(weight - means)
    wst[:64] = hi
    wst[64:] = lo

    for copy in ring1:
        copy.wait_recv()
    total = part[me8]
    for i in range(1, group8):
        total = total + got1[i]
    sum1[...] = total
    ring2 = []
    for i in range(1, DEPTHS):
        z = (depth + i) % DEPTHS
        copy = sent(sum1, got2.at[i], s2.at[i], g2.at[i], (wide_of(me8, z), n))
        copy.start()
        ring2.append(copy)

    for k, (src, dst, gives, gets, to) in enumerate(edges):

        @pl.when(gets)
        def _():
            edge_copies[k].wait_recv()

    lane1 = lax.broadcasted_iota(jnp.int32, (16, LANES), 1)
    pick = jnp.where(
        (lax.broadcasted_iota(jnp.int32, (32, LANES), 1) % 64) // 2
        == lax.broadcasted_iota(jnp.int32, (32, LANES), 0),
        1.0,
        0.0,
    ).astype(BF16)
    latents = []
    for h in range(rows):
        value = a_v[h + 1] + bm_v[h]
        if h == 0:
            value = value + (at_v[...] + bt_v[...])
        if h == rows - 1:
            value = value + (ab_v[...] + bb_v[...])
        latents.append(value)
    patches = []
    for p in range(pairs):
        blocks = []
        for t in range(2):
            for u in range(2):
                for v in range(2):
                    keep = jnp.logical_and(lane1 // 64 == t, lane1 % 2 == v)
                    blocks.append(jnp.where(keep, latents[2 * p + u], 0.0).astype(BF16))
        patches.append(dot_t(pick, jnp.concatenate(blocks, axis=0)))
    x = jnp.concatenate(patches, axis=0)
    x_all[n] = x.astype(BF16)
    ringx = []
    for i in range(1, narrows):
        copy = sent(x_all.at[n], x_all.at[n], sx.at[i], gx.at[i], (w, (n + i) % narrows))
        copy.start()
        ringx.append(copy)

    for copy in ring2:
        copy.wait_recv()
    total = sum1[...]
    for i in range(1, DEPTHS):
        total = total + got2[i]
    m_all[me8] = total[:, :768]
    e_out[...] = total[:, 768:]
    ring3 = []
    for i in range(1, group8):
        q = (me8 + i) % group8
        copy = sent(m_all.at[me8], m_all.at[me8], s3.at[i], g3.at[i], (wide_of(q, depth), n))
        copy.start()
        ring3.append(copy)

    per = x.shape[0]
    other = rolled(x, 64)
    low = lax.broadcasted_iota(jnp.int32, x.shape, 1) < 64
    twice = jnp.concatenate([jnp.where(low, x, other), jnp.where(low, other, x)], axis=0).astype(BF16)
    squares = jnp.zeros((2 * per, LANES), F32)
    step = 512
    for k in range(width // step):
        piece = pl.ds(k * step, step)
        centre = dot(twice, wst[:, piece]) + (pb_v[:, piece] - bias_mean)
        centre = centre * centre
        for i in range(step // LANES):
            squares = squares + centre[:, i * LANES : (i + 1) * LANES]
    spread = jnp.sum(squares, axis=1, keepdims=True) * (1.0 / width)
    factor = lax.rsqrt(spread + 1e-06)
    lane2 = lax.broadcasted_iota(jnp.int32, (per, LANES), 1)
    placed = jnp.where(lane2 == 0, factor[:per], jnp.where(lane2 == 1, factor[per:], 0.0))
    placed = jnp.concatenate([placed, jnp.zeros((LANES - per, LANES), F32)], axis=0)
    r_all[n] = jnp.transpose(placed)[:8]
    ringr = []
    for i in range(1, narrows):
        copy = sent(r_all.at[n], r_all.at[n], sr.at[i], gr.at[i], (w, (n + i) % narrows))
        copy.start()
        ringr.append(copy)

    for copy in ringx:
        copy.wait_recv()
    x_out[...] = x_all[...]
    for copy in ring3:
        copy.wait_recv()
    m_out[...] = m_all[...]
    for copy in ringr:
        copy.wait_recv()
    r_out[...] = r_all[...]
    for copy in ring1 + ring2 + ring3 + ringx + ringr:
        copy.wait_send()
    for k, (src, dst, gives, gets, to) in enumerate(edges):

        @pl.when(gives)
        def _():
            edge_copies[k].wait_send()


def back(x_ref, r_ref, m_ref, e_ref, bias, gains, out, xx, mm, factor, stage, sems):
    tokens = x_ref.shape[0]
    per = tokens // 8
    xx[:, :LANES] = x_ref[...]
    xx[:, LANES:] = x_ref[...]
    hi, lo = halves(m_ref[...])
    mm[...] = jnp.zeros(mm.shape, BF16)
    for t in range(2):
        mm[t, 64 * t : 64 * t + 64] = hi
        mm[t, 128 + 64 * t : 192 + 64 * t] = lo
    flat = r_ref[...]
    turned = jnp.transpose(jnp.concatenate([flat, jnp.zeros((LANES - flat.shape[0], LANES), F32)], axis=0))
    copies = []
    for t in range(2):
        for src in range(8):
            column = turned[:per, 8 * src + t : 8 * src + t + 1]
            factor[t, per * src : per * src + per] = jnp.broadcast_to(column, (per, LANES))
    for t in range(2):
        for j in range(3):
            product = dot(xx[...], mm[t, :, 256 * j : 256 * j + 256])
            rows_b = e_ref[2 * j : 2 * j + 1]
            rows_c = e_ref[2 * j + 1 : 2 * j + 2] + bias[j : j + 1]
            for hd in range(2):
                cols = slice(LANES * hd, LANES * hd + LANES)
                y = (product[:, cols] + rows_b[:, cols]) * factor[t] + rows_c[:, cols]
                if j < 2:
                    mean = jnp.sum(y * y, axis=1, keepdims=True) * (1.0 / LANES)
                    y = y * lax.rsqrt(mean + 1e-06) * gains[j : j + 1]
                stage[3 * t + j, :, cols] = y.astype(BF16)
            copy = pltpu.make_async_copy(
                stage.at[3 * t + j], out.at[j, pl.ds(t * tokens, tokens)], sems.at[3 * t + j]
            )
            copy.start()
            copies.append(copy)
    for copy in copies:
        copy.wait()


def local(wides, narrows, activations, conv_weight, patch_weight, patch_bias, shift, scale, qkv_weight, qkv_bias, norm_gains):
    rows, cols, channels = activations.shape[1:]
    width = patch_weight.shape[1]
    taps = jnp.transpose(conv_weight, (0, 1, 2, 4, 3)).reshape(-1, channels)
    qkv = jnp.transpose(qkv_weight, (1, 0, 2))
    group8 = wides // DEPTHS
    per = rows // 2 * cols // 2
    any_spec = pl.BlockSpec(memory_space=pl.ANY)
    vmem = pl.BlockSpec(memory_space=pltpu.VMEM)
    dma = pltpu.SemaphoreType.DMA
    edge = pltpu.VMEM((16, LANES), F32)
    x, r, m, e = pl.pallas_call(
        functools.partial(front, (wides, narrows, rows, width)),
        out_shape=[
            jax.ShapeDtypeStruct((narrows, per, LANES), BF16),
            jax.ShapeDtypeStruct((narrows, 8, LANES), F32),
            jax.ShapeDtypeStruct((8, 8, 768), F32),
            jax.ShapeDtypeStruct((8, 256), F32),
        ],
        in_specs=[any_spec] * 7,
        out_specs=[vmem] * 4,
        scratch_shapes=[
            pltpu.VMEM((rows, 2, cols, channels), BF16),
            pltpu.VMEM(taps.shape, BF16),
            pltpu.VMEM(patch_weight.shape, BF16),
            pltpu.VMEM((1, width), F32),
            pltpu.VMEM((1, width), F32),
            pltpu.VMEM((1, width), F32),
            pltpu.VMEM((3, LANES, 256), BF16),
            pltpu.VMEM((group8, 8, 1024), F32),
            pltpu.VMEM((group8, 8, 1024), F32),
            pltpu.VMEM((8, 1024), F32),
            pltpu.VMEM((DEPTHS, 8, 1024), F32),
            pltpu.VMEM((8, 1024), F32),
            pltpu.VMEM((8, 8, 768), F32),
            pltpu.VMEM((rows, taps.shape[0], LANES), F32),
            pltpu.VMEM((rows + 2, 16, LANES), F32),
            pltpu.VMEM((rows + 2, 16, LANES), F32),
            edge,
            edge,
            pltpu.VMEM((rows, 16, LANES), F32),
            edge,
            edge,
            pltpu.VMEM((LANES, width), BF16),
            pltpu.VMEM((narrows, per, LANES), BF16),
            pltpu.VMEM((narrows, 8, LANES), F32),
            dma((6,)),
            dma((rows,)),
            dma((group8,)),
            dma((group8,)),
            dma((DEPTHS,)),
            dma((DEPTHS,)),
            dma((group8,)),
            dma((group8,)),
            dma((narrows,)),
            dma((narrows,)),
            dma((narrows,)),
            dma((narrows,)),
            dma((5,)),
            dma((5,)),
        ],
        compiler_params=pltpu.CompilerParams(
            collective_id=0, has_side_effects=True, vmem_limit_bytes=40 * 1024 * 1024
        ),
        name="front",
    )(
        activations,
        taps,
        patch_weight,
        patch_bias.reshape(1, -1),
        shift.reshape(1, -1),
        scale.reshape(1, -1),
        qkv,
    )
    tokens = narrows * per
    return pl.pallas_call(
        back,
        out_shape=jax.ShapeDtypeStruct((3, 2 * tokens, 256), BF16),
        in_specs=[vmem] * 6,
        out_specs=any_spec,
        scratch_shapes=[
            pltpu.VMEM((tokens, 2 * LANES), BF16),
            pltpu.VMEM((2, 256, 768), BF16),
            pltpu.VMEM((2, tokens, LANES), F32),
            pltpu.VMEM((6, tokens, 256), BF16),
            dma((6,)),
        ],
        compiler_params=pltpu.CompilerParams(vmem_limit_bytes=40 * 1024 * 1024),
        name="back",
    )(x.reshape(tokens, LANES), r.reshape(narrows * 8, LANES), m.reshape(64, 768), e, qkv_bias, norm_gains)


def solution(mesh):
    placed = (
        P("wide", "narrow", None, None),
        P(),
        P(),
        P(),
        P(),
        P(),
        P("wide", None, "narrow"),
        P(None, "narrow"),
        P(),
    )
    return jax.shard_map(
        functools.partial(local, mesh.shape["wide"], mesh.shape["narrow"]),
        mesh=mesh,
        in_specs=placed,
        out_specs=P(None, "wide", "narrow"),
        check_vma=False,
    )
```

time: 300 us -> 38.5 us (0.13)
  waiting for transfers between devices: 241 us -> 0 us
  Pallas kernels: 0 us -> 30.6 us
  matrix products: 14.1 us -> 0 us
  between operations: 13.6 us -> 0.03 us
  starting transfers between devices: 12.2 us -> 0 us
  other arithmetic: 7.25 us -> 0 us
  local copies, waits for them, and re-layouts: 11.5 us -> 7.53 us
    all_gather x2 -> x0, waiting for transfers between devices: 217 us -> none  [the longest x1 183 us: local(): group = lax.all_gather(features, 'narrow', axis=1, tiled=True)]
    pallas_call x0 -> x2, Pallas kernels: none -> 30.6 us  [the longest x1 27.9 us: local(): pl.pallas_call(functools.partial(front, (wides, narrows, rows, width)), o...]
    ppermute x3 -> x0, waiting for transfers between devices: 23.3 us -> none  [the longest x1 18.3 us: shifted(): return lax.ppermute(x, axis, pairs)]
    dot_general x3 -> x0, matrix products: 14.1 us -> none  [the longest x1 11.5 us: local(): jnp.dot(group, piece.reshape(piece.shape[0], column_count), preferred_ele...]
    ppermute x3 -> x0, starting transfers between devices: 12.1 us -> none  [the longest x1 6.47 us: shifted(): return lax.ppermute(x, axis, pairs)]
    all_gather x1 -> x0, local copies, waits for them, and re-layouts: 6.66 us -> none  [local(): piece = lax.all_gather(qkv_weight, 'wide', axis=0, tiled=True)]
    unnamed x18, local copies, waits for them, and re-layouts: 1.06 us -> 7.53 us
    convert_element_type x3 -> x0, other arithmetic: 3.25 us -> none  [the longest x1 1.59 us: local(): acted = jax.nn.silu(activations.astype(jnp.float32)).astype(jnp.bfloat16)]
  transfers between devices with their start and end apart: 5 -> 0, of which waited for: 5 -> 0; matrix products, arithmetic and copies ran while one was open for 5% -> 0% of each run, Pallas kernels for 0% -> 0%
where the time goes in v1:
time: 38.5 us; the launch traced here: 38.1 us
  Pallas kernels  30.6 us (79%)
  local copies, waits for them, and re-layouts  7.53 us (20%)
    pallas_call x1, Pallas kernels, local(): pl.pallas_call(functools.partial(front, (wides, narrows, rows, width)), o...  27.9 us
    unnamed x18, local copies, waits for them, and re-layouts  7.53 us
    pallas_call x1, Pallas kernels, local(): pl.pallas_call(back, out_shape=jax.ShapeDtypeStruct((3, 2 * tokens, 256),...  2.64 us

profile of v1, /device:TPU:1, one launch (start us, length us, event | category | flops | bytes accessed | tf_op | source)
XLA Modules:
  0.0 38.1 jit_solution(14203818699664797535)
XLA Ops:
  0.0 0.0 copy-start
  0.0 1.1 %copy-done = bf16[2,6,64,512]{3,2,1,0:T(8,128)(2,1)S(1)} copy-done((bf16[2,6,64,512]{3,2,1,0:T(8,128)(2,1)S(1)}, bf16[2,6,64,512]{3,2,1,0:T(8,128)(2,1)}, u32[]{:S(2)}) %copy-start) | copy-done | bytes 786456
  1.1 0.0 copy-start.1
  1.1 1.0 %copy-done.1 = bf16[3,3,3,512,16]{3,4,2,1,0:T(8,128)(2,1)S(1)} copy-done((bf16[3,3,3,512,16]{3,4,2,1,0:T(8,128)(2,1)S(1)}, bf16[3,3,3,512,16]{3,4,2,1,0:T(8,128)(2,1)}, u32[]{:S(2)}) %copy-start.1) | copy-done | bytes 442392
  2.1 0.0 copy-start.2
  2.1 1.0 %copy-done.2 = bf16[64,3072]{1,0:T(8,128)(2,1)S(1)} copy-done((bf16[64,3072]{1,0:T(8,128)(2,1)S(1)}, bf16[64,3072]{1,0:T(8,128)(2,1)}, u32[]{:S(2)}) %copy-start.2) | copy-done | bytes 393240
  3.1 0.0 copy-start.3
  3.1 0.9 %copy-done.3 = bf16[96,3,256]{2,0,1:T(8,128)(2,1)S(1)} copy-done((bf16[96,3,256]{2,0,1:T(8,128)(2,1)S(1)}, bf16[96,3,256]{2,0,1:T(8,128)(2,1)}, u32[]{:S(2)}) %copy-start.3) | copy-done | bytes 147480
  4.1 0.0 copy-start.4
  4.1 0.7 %copy-done.4 = f32[3072]{0:T(1024)S(1)} copy-done((f32[3072]{0:T(1024)S(1)}, f32[3072]{0:T(1024)}, u32[]{:S(2)}) %copy-start.4) | copy-done | bytes 12312
  4.8 0.0 copy-start.5
  4.8 0.7 %copy-done.5 = f32[3072]{0:T(1024)S(1)} copy-done((f32[3072]{0:T(1024)S(1)}, f32[3072]{0:T(1024)}, u32[]{:S(2)}) %copy-start.5) | copy-done | bytes 12312
  5.5 0.0 copy-start.6
  5.5 0.7 %copy-done.6 = f32[3072]{0:T(1024)S(1)} copy-done((f32[3072]{0:T(1024)S(1)}, f32[3072]{0:T(1024)}, u32[]{:S(2)}) %copy-start.6) | copy-done | bytes 12312
  6.2 27.9 %front.1 = (bf16[8,96,128]{2,1,0:T(8,128)(2,1)S(1)}, f32[8,8,128]{2,1,0:T(8,128)S(1)}, f32[8,8,768]{2,1,0:T(8,128)S(1)}, f32[8,256]{1,0:T(8,128)S(1)}) custom-call(bf16[2,6,64,512]{3,2,1,0:T(8,128)(2,1)S(1)} %copy-done, bf16[432,512]{1,0:T(8,128)(2,1)S(1)} %bitcast.10, bf16[64,3072]{1,0:T(8,128)(2,1)S(1)} %copy-done.2, f32[1,3072]{1,0:T(1,128)S(1)} %bitcast.15, ...), custom_call_target="tpu_custom_call" | custom-call | tf_op jit(solution)/shard_map/front/pallas_call | solution.py:372
  34.1 0.0 copy-start.7
  34.1 0.7 %copy-done.7 = f32[3,256]{1,0:T(4,128)S(1)} copy-done((f32[3,256]{1,0:T(4,128)S(1)}, f32[3,256]{1,0:T(4,128)}, u32[]{:S(2)}) %copy-start.7) | copy-done | bytes 3096
  34.8 0.0 copy-start.8
  34.8 0.7 %copy-done.8 = f32[2,128]{1,0:T(2,128)S(1)} copy-done((f32[2,128]{1,0:T(2,128)S(1)}, f32[2,128]{1,0:T(2,128)}, u32[]{:S(2)}) %copy-start.8) | copy-done | bytes 1048
  35.5 2.6 %back.1 = bf16[3,1536,256]{2,1,0:T(8,128)(2,1)} custom-call(bf16[768,128]{1,0:T(8,128)(2,1)S(1)} %bitcast.11, f32[64,128]{1,0:T(8,128)S(1)} %bitcast.14, f32[64,768]{1,0:T(8,128)S(1)} %bitcast.12, f32[8,256]{1,0:T(8,128)S(1)} %get-tuple-element.12.e_ref, f32[3,256]{1,0:T(4,128)S(1)} %copy-done.7, f32[2,128]{1,0:T(2,128)S(1)} %copy-done.8), custom_call_target="tpu_custom_call" | custom-call | tf_op jit(solution)/shard_map/back/pallas_call | solution.py:436
Async XLA Ops:
  0.0 1.1 %copy-start = (bf16[2,6,64,512]{3,2,1,0:T(8,128)(2,1)S(1)}, bf16[2,6,64,512]{3,2,1,0:T(8,128)(2,1)}, u32[]{:S(2)}) copy-start(bf16[2,6,64,512]{3,2,1,0:T(8,128)(2,1)} %act.1) | copy-start | bytes 2359300
  1.1 1.0 %copy-start.1 = (bf16[3,3,3,512,16]{3,4,2,1,0:T(8,128)(2,1)S(1)}, bf16[3,3,3,512,16]{3,4,2,1,0:T(8,128)(2,1)}, u32[]{:S(2)}) copy-start(bf16[3,3,3,512,16]{3,4,2,1,0:T(8,128)(2,1)} %param.10) | copy-start | bytes 1327108
  2.1 1.0 %copy-start.2 = (bf16[64,3072]{1,0:T(8,128)(2,1)S(1)}, bf16[64,3072]{1,0:T(8,128)(2,1)}, u32[]{:S(2)}) copy-start(bf16[64,3072]{1,0:T(8,128)(2,1)} %pw.1) | copy-start | bytes 1179652
  3.1 0.9 %copy-start.3 = (bf16[96,3,256]{2,0,1:T(8,128)(2,1)S(1)}, bf16[96,3,256]{2,0,1:T(8,128)(2,1)}, u32[]{:S(2)}) copy-start(bf16[96,3,256]{2,0,1:T(8,128)(2,1)} %param.15) | copy-start | bytes 442372
  4.1 0.7 %copy-start.4 = (f32[3072]{0:T(1024)S(1)}, f32[3072]{0:T(1024)}, u32[]{:S(2)}) copy-start(f32[3072]{0:T(1024)} %param.12) | copy-start | bytes 36868
  4.8 0.7 %copy-start.5 = (f32[3072]{0:T(1024)S(1)}, f32[3072]{0:T(1024)}, u32[]{:S(2)}) copy-start(f32[3072]{0:T(1024)} %param.13) | copy-start | bytes 36868
  5.5 0.7 %copy-start.6 = (f32[3072]{0:T(1024)S(1)}, f32[3072]{0:T(1024)}, u32[]{:S(2)}) copy-start(f32[3072]{0:T(1024)} %param.14) | copy-start | bytes 36868
  34.1 0.7 %copy-start.7 = (f32[3,256]{1,0:T(4,128)S(1)}, f32[3,256]{1,0:T(4,128)}, u32[]{:S(2)}) copy-start(f32[3,256]{1,0:T(4,128)} %bias.1) | copy-start | bytes 9220
  34.8 0.7 %copy-start.8 = (f32[2,128]{1,0:T(2,128)S(1)}, f32[2,128]{1,0:T(2,128)}, u32[]{:S(2)}) copy-start(f32[2,128]{1,0:T(2,128)} %gains.1) | copy-start | bytes 3076

commit v2 on v1

v2 whole, which is shorter than its diff:
```python
import functools

import jax
import jax.numpy as jnp
from jax import lax
from jax.experimental import pallas as pl
from jax.experimental.pallas import tpu as pltpu
from jax.sharding import PartitionSpec as P

MESH = pl.DeviceIdType.MESH
F32 = jnp.float32
BF16 = jnp.bfloat16
DEPTHS = 4
CORES = 2
LANES = 128


def rolled(x, by):
    return pltpu.roll(x, by % x.shape[1], 1)


def halves(x):
    high = x.astype(BF16)
    return high, (x - high.astype(F32)).astype(BF16)


def dot(a, b):
    return lax.dot_general(a, b, (((1,), (0,)), ((), ())), preferred_element_type=F32)


def dot_t(a, b):
    return lax.dot_general(a, b, (((1,), (1,)), ((), ())), preferred_element_type=F32)


def front(
    sizes,
    act, cw, pw, pb, sh, sc, qw, qb, ng,
    x_out, m_out, e_out,
    act_v, cw_v, pw_v, pb_v, sh_v, sc_v, qw_v, qb_v, ng_v,
    part, pair, share, got1, own, got2, m_all, prod,
    a_v, b_v, at_v, ab_v, bm_v, bt_v, bb_v,
    wst, x_all, r_all,
    in_sem, act_sem, s0, g0, s1, g1, s3, g3, sx, gx, sh_sem, gh_sem,
):
    wides, narrows, rows, width = sizes
    span = qw.shape[1]
    w = lax.axis_index("wide")
    n = lax.axis_index("narrow")
    pairs = rows // 2
    chips = wides // CORES
    core = w % CORES
    me = w // CORES
    partner = w + 1 - 2 * core
    sums = core == CORES - 1

    chip_y = me // DEPTHS
    chip_z = me % DEPTHS
    highs = chips // DEPTHS
    each = share.shape[1]

    def core1(y, z):
        return (y % highs * DEPTHS + z % DEPTHS) * CORES + CORES - 1, n

    def landed(ref, sem):
        pltpu.make_async_copy(ref, ref, sem).wait()

    loads = []
    for k, (src, dst) in enumerate(
        [(pw, pw_v), (sc, sc_v), (sh, sh_v), (pb, pb_v), (qw, qw_v.at[:, pl.ds(0, span), :]), (cw, cw_v), (qb, qb_v), (ng, ng_v)]
    ):
        copy = pltpu.make_async_copy(src, dst, in_sem.at[k])
        copy.start()
        loads.append(copy)
    for k in range(pairs):
        for t in range(2):
            pltpu.make_async_copy(
                act.at[t, pl.ds(2 * k, 2)], act_v.at[pl.ds(2 * k, 2), t], act_sem.at[k]
            ).start()

    barrier = pltpu.get_barrier_semaphore()

    def greet(wide, narrow):
        pl.semaphore_signal(barrier, inc=1, device_id=(wide, narrow), device_id_type=MESH)

    @pl.when(sums)
    def _():
        for i in range(1, DEPTHS):
            greet(*core1(chip_y, chip_z + i))
        for i in range(1, highs):
            greet(*core1(chip_y + i, chip_z))

    for i in range(1, narrows):
        greet(w, (n + i) % narrows)
    has_next = w < wides - 1
    has_prev = w > 0
    for there, dw in ((has_next, 1), (has_prev, -1)):
        for dn in (-1, 0, 1):
            inside = there
            if dn == -1:
                inside = jnp.logical_and(there, n > 0)
            if dn == 1:
                inside = jnp.logical_and(there, n < narrows - 1)

            @pl.when(inside)
            def _():
                greet(w + dw, n + dn)

    greet(partner, n)
    sides = jnp.where(has_next, 1, 0) + jnp.where(has_prev, 1, 0)
    across = 1 + jnp.where(n > 0, 1, 0) + jnp.where(n < narrows - 1, 1, 0)
    expected = jnp.where(sums, DEPTHS + highs - 1, 1) + (narrows - 1) + sides * across

    qw_v[:, span:, :] = jnp.zeros((3, qw_v.shape[1] - span, qw_v.shape[2]), BF16)
    for copy in loads[:5]:
        copy.wait()
    weight = pw_v[...].astype(F32)
    means = jnp.sum(weight, axis=1, keepdims=True) * (1.0 / width)
    bias_mean = jnp.sum(pb_v[...], axis=1, keepdims=True) * (1.0 / width)
    begin = w * span
    base = pl.multiple_of(jnp.minimum(begin // LANES, width // LANES - 2) * LANES, LANES)
    window = pl.ds(base, 2 * LANES)
    gain = 1.0 + sc_v[:, window]
    main = (pw_v[:, window].astype(F32) - means) * gain
    extra_b = (pb_v[:, window] - bias_mean) * gain
    extra_s = sh_v[:, window]
    pad = jnp.zeros((14, 2 * LANES), F32)
    stacked = jnp.concatenate([main, extra_b, extra_s, pad], axis=0)
    shift_by = (2 * LANES - (begin - base)) % (2 * LANES)
    stacked = pltpu.roll(stacked, shift_by, 1)[:, :LANES]
    lane = lax.broadcasted_iota(jnp.int32, stacked.shape, 1)
    stacked = jnp.where(lane < span, stacked, 0.0)
    hi, lo = halves(stacked)
    for j in range(3):
        res = dot(hi, qw_v[j]) + dot(lo, qw_v[j])
        for head in range(2):
            part[15 * head + 5 * j : 15 * head + 5 * j + 5] = res[:, head * LANES : (head + 1) * LANES].reshape(5, 16, LANES)
    loads[5].wait()
    for k in range(pairs):
        landed(act_v.at[pl.ds(2 * k, 2)], act_sem.at[k])
        raw = act_v[2 * k : 2 * k + 2].reshape(256, act.shape[3]).astype(F32)
        acted = (raw / (1.0 + jnp.exp(-raw))).astype(BF16)
        res = dot_t(cw_v[...], acted)
        prod[2 * k] = res[:, :LANES]
        prod[2 * k + 1] = res[:, LANES:]

    full = (16 * (rows + 2), LANES)
    col = lax.broadcasted_iota(jnp.int32, full, 1) % 64
    early = lax.broadcasted_iota(jnp.int32, full, 1) < 64
    taps = []
    for a in range(3):
        moved = []
        for c in range(3):
            planes = []
            for h in range(-1, rows + 1):
                total = None
                for b in range(3):
                    src = h + b - 1
                    if 0 <= src < rows:
                        g = (a * 3 + b) * 3 + c
                        piece = prod[src, 16 * g : 16 * g + 16, :]
                        total = piece if total is None else total + piece
                planes.append(total)
            moved.append(jnp.concatenate(planes, axis=0))
        left = jnp.where(col == 0, 0.0, rolled(moved[0], 1))
        right = jnp.where(col == 63, 0.0, rolled(moved[2], -1))
        taps.append(moved[1] + left + right)
    swapped = rolled(taps[1], 64)
    here = taps[2] + jnp.where(early, 0.0, swapped)
    ahead = taps[0] + jnp.where(early, swapped, 0.0)
    copies = jnp.where(early, taps[1] + taps[0], rolled(taps[0], 64))
    here = here + jnp.where(w == 0, copies, 0.0)
    a_v[...] = here.reshape(rows + 2, 16, LANES)
    b_v[...] = ahead.reshape(rows + 2, 16, LANES)

    pl.semaphore_wait(barrier, expected)

    def sent(src, dst, ssem, gsem, to):
        return pltpu.make_async_remote_copy(
            src_ref=src, dst_ref=dst, send_sem=ssem, recv_sem=gsem, device_id=to, device_id_type=MESH
        )

    pair_copy = sent(part, pair, s0.at[0], g0.at[0], (partner, n))

    @pl.when(jnp.logical_not(sums))
    def _():
        pair_copy.start()

    up = n > 0
    down = n < narrows - 1
    edges = [
        (b_v.at[pl.ds(1, rows)], bm_v, has_next, has_prev, (w + 1, n)),
        (a_v.at[0], ab_v, up, down, (w, n - 1)),
        (a_v.at[rows + 1], at_v, down, up, (w, n + 1)),
        (b_v.at[0], bb_v, jnp.logical_and(has_next, up), jnp.logical_and(has_prev, down), (w + 1, n - 1)),
        (b_v.at[rows + 1], bt_v, jnp.logical_and(has_next, down), jnp.logical_and(has_prev, up), (w + 1, n + 1)),
    ]
    edge_copies = []
    for k, (src, dst, gives, gets, to) in enumerate(edges):
        copy = sent(src, dst, sh_sem.at[k], gh_sem.at[k], to)
        edge_copies.append(copy)

        @pl.when(gives)
        def _():
            copy.start()

        @pl.when(jnp.logical_not(gets))
        def _():
            dst[...] = jnp.zeros(dst.shape, F32)

    hi, lo = halves(weight - means)
    wst[:64] = hi
    wst[64:] = lo

    row16 = lax.broadcasted_iota(jnp.int32, (16, LANES), 0)
    last = sent(m_all, m_all, s3.at[0], g3.at[0], (partner, n))

    @pl.when(sums)
    def _():
        pair_copy.wait_recv()
        for tile in range(30):
            total = part[tile] + pair[tile]
            if tile % 5 == 4:
                hi = total.astype(BF16).astype(F32)
                total = jnp.where(row16 < 2, hi, pltpu.roll(total - hi, 2, 0))
            share[tile // each, tile % each] = total.astype(BF16)
        for tile in range(30, highs * each):
            share[tile // each, tile % each] = jnp.zeros((16, LANES), BF16)
        for i in range(1, highs):
            sent(
                share.at[(chip_y + i) % highs], got1.at[i - 1], s1.at[0], g1.at[0], core1(chip_y + i, chip_z)
            ).start()

    @pl.when(sums)
    def _():
        landed(got1, g1.at[0])
        total = share[chip_y].astype(F32)
        for i in range(1, highs):
            total = total + got1[i - 1].astype(F32)
        own[...] = total.astype(BF16)
        for i in range(1, DEPTHS):
            sent(own, got2.at[i - 1], s1.at[1], g1.at[1], core1(chip_y, chip_z + i)).start()

    for k, (src, dst, gives, gets, to) in enumerate(edges):

        @pl.when(gets)
        def _():
            edge_copies[k].wait_recv()

    lane1 = lax.broadcasted_iota(jnp.int32, (16, LANES), 1)
    pick = jnp.where(
        (lax.broadcasted_iota(jnp.int32, (32, LANES), 1) % 64) // 2
        == lax.broadcasted_iota(jnp.int32, (32, LANES), 0),
        1.0,
        0.0,
    ).astype(BF16)
    latents = []
    for h in range(rows):
        value = a_v[h + 1] + bm_v[h]
        if h == 0:
            value = value + (at_v[...] + bt_v[...])
        if h == rows - 1:
            value = value + (ab_v[...] + bb_v[...])
        latents.append(value)
    patches = []
    for p in range(pairs):
        blocks = []
        for t in range(2):
            for u in range(2):
                for v in range(2):
                    keep = jnp.logical_and(lane1 // 64 == t, lane1 % 2 == v)
                    blocks.append(jnp.where(keep, latents[2 * p + u], 0.0).astype(BF16))
        patches.append(dot_t(pick, jnp.concatenate(blocks, axis=0)))
    x = jnp.concatenate(patches, axis=0)
    x_all[n] = x.astype(BF16)
    for i in range(1, narrows):
        sent(x_all.at[n], x_all.at[n], sx.at[0], gx.at[0], (w, (n + i) % narrows)).start()

    per = x.shape[0]
    other = rolled(x, 64)
    low = lax.broadcasted_iota(jnp.int32, x.shape, 1) < 64
    twice = jnp.concatenate([jnp.where(low, x, other), jnp.where(low, other, x)], axis=0).astype(BF16)
    squares = jnp.zeros((2 * per, LANES), F32)
    step = 512
    for k in range(width // step):
        piece = pl.ds(k * step, step)
        centre = dot(twice, wst[:, piece]) + (pb_v[:, piece] - bias_mean)
        centre = centre * centre
        for i in range(step // LANES):
            squares = squares + centre[:, i * LANES : (i + 1) * LANES]
    spread = jnp.sum(squares, axis=1, keepdims=True) * (1.0 / width)
    factor = lax.rsqrt(spread + 1e-06)
    lane2 = lax.broadcasted_iota(jnp.int32, (per, LANES), 1)
    placed = jnp.where(lane2 == 0, factor[:per], jnp.where(lane2 == 1, factor[per:], 0.0))
    placed = jnp.concatenate([placed, jnp.zeros((LANES - per, LANES), F32)], axis=0)
    r_all[n] = jnp.transpose(placed)[:8]
    for i in range(1, narrows):
        sent(r_all.at[n], r_all.at[n], sx.at[1], gx.at[1], (w, (n + i) % narrows)).start()

    mine = m_all.at[pl.ds(each * chip_y, each)]

    @pl.when(sums)
    def _():
        landed(got2, g1.at[1])
        total = own[...].astype(F32)
        for i in range(1, DEPTHS):
            total = total + got2[i - 1].astype(F32)
        for k in range(each):
            plain = total[k]
            both = plain + pltpu.roll(plain, 14, 0)
            hi = both.astype(BF16).astype(F32)
            both = jnp.where(row16 < 2, hi, pltpu.roll(both - hi, 2, 0))
            tile = each * chip_y + k
            m_all[tile] = jnp.where(tile % 5 == 4, both, plain).astype(BF16)
        for i in range(1, highs):
            sent(mine, mine, s1.at[2], g1.at[2], core1(chip_y + i, chip_z)).start()

    loads[6].wait()
    loads[7].wait()
    e_out[0:3] = qb_v[...]
    e_out[3:5, :LANES] = ng_v[...]
    landed(x_all.at[pl.ds(0, narrows - 1)], gx.at[0])
    landed(r_all.at[pl.ds(0, narrows - 1)], gx.at[1])
    flat = r_all[...].reshape(narrows * 8, LANES)
    turned = jnp.transpose(jnp.concatenate([flat, jnp.zeros((LANES - narrows * 8, LANES), F32)], axis=0))
    for src in range(narrows):
        theirs = x_all[src].astype(F32)
        for t in range(2):
            column = turned[:per, 8 * src + t : 8 * src + t + 1]
            value = theirs * column
            hi = value.astype(BF16).astype(F32)
            lo = value - hi
            value = jnp.where(low, hi, rolled(lo, 64)) if t == 0 else jnp.where(low, rolled(hi, 64), lo)
            hi = column.astype(BF16).astype(F32)
            more = jnp.where(lane2 == 1, column - hi, jnp.where(lane2 < 3, hi, jnp.where(lane2 < 5, 1.0, 0.0)))
            place = pl.ds((t * narrows + src) * per, per)
            x_out[place, :LANES] = value.astype(BF16)
            x_out[place, LANES:] = more.astype(BF16)
    @pl.when(sums)
    def _():
        landed(m_all.at[pl.ds(0, each * (highs - 1))], g1.at[2])
        last.start()

    @pl.when(jnp.logical_not(sums))
    def _():
        last.wait_recv()

    m_out[...] = m_all[...]
    landed(x_all.at[pl.ds(0, narrows - 1)], sx.at[0])
    landed(r_all.at[pl.ds(0, narrows - 1)], sx.at[1])

    @pl.when(sums)
    def _():
        landed(got1, s1.at[0])
        landed(got2, s1.at[1])
        landed(m_all.at[pl.ds(0, each * (highs - 1))], s1.at[2])
        last.wait_send()

    @pl.when(jnp.logical_not(sums))
    def _():
        pair_copy.wait_send()

    for k, (src, dst, gives, gets, to) in enumerate(edges):

        @pl.when(gives)
        def _():
            edge_copies[k].wait_send()


def back(x_ref, m_ref, e_ref, out, mm, stage, sems):
    tokens = x_ref.shape[0] // 2
    row16 = lax.broadcasted_iota(jnp.int32, (16, LANES), 0)
    mm[144:] = jnp.zeros((112, 768), BF16)
    for head in range(2):
        for j in range(3):
            cols = slice(256 * j + LANES * head, 256 * j + LANES * (head + 1))
            tile = 15 * head + 5 * j
            block = m_ref[tile : tile + 4].reshape(64, LANES)
            mm[:64, cols] = block
            mm[64:128, cols] = block
            extra = m_ref[tile + 4].astype(F32)
            constant = extra[1:2] + extra[3:4] + e_ref[j : j + 1, LANES * head : LANES * (head + 1)]
            high = constant.astype(BF16).astype(F32)
            rows = jnp.where(row16 < 2, extra[0:1], 0.0)
            rows = jnp.where(row16 == 2, extra[2:3], rows)
            rows = jnp.where(row16 == 3, high, rows)
            rows = jnp.where(row16 == 4, constant - high, rows)
            mm[128:144, cols] = rows.astype(BF16)
    copies = []
    for t in range(2):
        for j in range(3):
            product = dot(x_ref[t * tokens : (t + 1) * tokens], mm[:, 256 * j : 256 * j + 256])
            for hd in range(2):
                cols = slice(LANES * hd, LANES * hd + LANES)
                y = product[:, cols]
                if j < 2:
                    mean = jnp.sum(y * y, axis=1, keepdims=True) * (1.0 / LANES)
                    y = y * lax.rsqrt(mean + 1e-06) * e_ref[3 + j : 4 + j, :LANES]
                stage[3 * t + j, :, cols] = y.astype(BF16)
            copy = pltpu.make_async_copy(
                stage.at[3 * t + j], out.at[j, pl.ds(t * tokens, tokens)], sems.at[3 * t + j]
            )
            copy.start()
            copies.append(copy)
    for copy in copies:
        copy.wait()


def local(wides, narrows, activations, conv_weight, patch_weight, patch_bias, shift, scale, qkv_weight, qkv_bias, norm_gains):
    rows, cols, channels = activations.shape[1:]
    width = patch_weight.shape[1]
    taps = jnp.transpose(conv_weight, (0, 1, 2, 4, 3)).reshape(-1, channels)
    qkv = jnp.transpose(qkv_weight, (1, 0, 2))
    highs = wides // (CORES * DEPTHS)
    each = -(-30 // highs)
    per = rows // 2 * cols // 2
    any_spec = pl.BlockSpec(memory_space=pltpu.HBM)
    vmem = pl.BlockSpec(memory_space=pltpu.VMEM)
    dma = pltpu.SemaphoreType.DMA
    edge = pltpu.VMEM((16, LANES), F32)
    x, m, e = pl.pallas_call(
        functools.partial(front, (wides, narrows, rows, width)),
        out_shape=[
            jax.ShapeDtypeStruct((2 * narrows * per, 2 * LANES), BF16),
            jax.ShapeDtypeStruct((highs * each, 16, LANES), BF16),
            jax.ShapeDtypeStruct((8, 256), F32),
        ],
        in_specs=[any_spec] * 9,
        out_specs=[vmem] * 3,
        scratch_shapes=[
            pltpu.VMEM((rows, 2, cols, channels), BF16),
            pltpu.VMEM(taps.shape, BF16),
            pltpu.VMEM(patch_weight.shape, BF16),
            pltpu.VMEM((1, width), F32),
            pltpu.VMEM((1, width), F32),
            pltpu.VMEM((1, width), F32),
            pltpu.VMEM((3, LANES, 256), BF16),
            pltpu.VMEM(qkv_bias.shape, F32),
            pltpu.VMEM(norm_gains.shape, F32),
            pltpu.VMEM((30, 16, LANES), F32),
            pltpu.VMEM((30, 16, LANES), F32),
            pltpu.VMEM((highs, each, 16, LANES), BF16),
            pltpu.VMEM((highs - 1, each, 16, LANES), BF16),
            pltpu.VMEM((each, 16, LANES), BF16),
            pltpu.VMEM((DEPTHS - 1, each, 16, LANES), BF16),
            pltpu.VMEM((highs * each, 16, LANES), BF16),
            pltpu.VMEM((rows, taps.shape[0], LANES), F32),
            pltpu.VMEM((rows + 2, 16, LANES), F32),
            pltpu.VMEM((rows + 2, 16, LANES), F32),
            edge,
            edge,
            pltpu.VMEM((rows, 16, LANES), F32),
            edge,
            edge,
            pltpu.VMEM((LANES, width), BF16),
            pltpu.VMEM((narrows, per, LANES), BF16),
            pltpu.VMEM((narrows, 8, LANES), F32),
            dma((8,)),
            dma((rows // 2,)),
            dma((1,)),
            dma((1,)),
            dma((3,)),
            dma((3,)),
            dma((1,)),
            dma((1,)),
            dma((2,)),
            dma((2,)),
            dma((5,)),
            dma((5,)),
        ],
        compiler_params=pltpu.CompilerParams(
            collective_id=0, has_side_effects=True, vmem_limit_bytes=40 * 1024 * 1024
        ),
        name="front",
    )(
        *(
            pltpu.with_memory_space_constraint(a, pltpu.HBM)
            for a in (
                activations,
                taps,
                patch_weight,
                patch_bias.reshape(1, -1),
                shift.reshape(1, -1),
                scale.reshape(1, -1),
                qkv,
                qkv_bias,
                norm_gains,
            )
        )
    )
    tokens = narrows * per
    return pl.pallas_call(
        back,
        out_shape=jax.ShapeDtypeStruct((3, 2 * tokens, 256), BF16),
        in_specs=[vmem] * 3,
        out_specs=any_spec,
        scratch_shapes=[
            pltpu.VMEM((2 * LANES, 768), BF16),
            pltpu.VMEM((6, tokens, 256), BF16),
            dma((6,)),
        ],
        compiler_params=pltpu.CompilerParams(vmem_limit_bytes=40 * 1024 * 1024),
        name="back",
    )(x, m, e)


def solution(mesh):
    placed = (
        P("wide", "narrow", None, None),
        P(),
        P(),
        P(),
        P(),
        P(),
        P("wide", None, "narrow"),
        P(None, "narrow"),
        P(),
    )
    return jax.shard_map(
        functools.partial(local, mesh.shape["wide"], mesh.shape["narrow"]),
        mesh=mesh,
        in_specs=placed,
        out_specs=P(None, "wide", "narrow"),
        check_vma=False,
    )
```

time: 38.5 us -> 26.5 us (0.69)
  local copies, waits for them, and re-layouts: 7.53 us -> 0 us
  Pallas kernels: 30.6 us -> 26.4 us
    unnamed x18 -> x0, local copies, waits for them, and re-layouts: 7.53 us -> none
    pallas_call x1, Pallas kernels: 27.9 us -> 24.2 us  [local(): pl.pallas_call(functools.partial(front, (wides, narrows, rows, width)), o...]
    pallas_call x1, Pallas kernels: 2.64 us -> 2.17 us  [local(): pl.pallas_call(back, out_shape=jax.ShapeDtypeStruct((3, 2 * tokens, 256),...]
where the time goes in v2:
time: 26.5 us; the launch traced here: 26.4 us
  Pallas kernels  26.4 us (100%)
    pallas_call x1, Pallas kernels, local(): pl.pallas_call(functools.partial(front, (wides, narrows, rows, width)), o...  24.2 us
    pallas_call x1, Pallas kernels, local(): pl.pallas_call(back, out_shape=jax.ShapeDtypeStruct((3, 2 * tokens, 256),...  2.17 us

profile of v2, /device:TPU:1, one launch (start us, length us, event | category | flops | bytes accessed | tf_op | source)
XLA Modules:
  0.0 26.4 jit_solution(15135640578380881305)
XLA Ops:
  0.0 24.2 %front.1 = (bf16[1536,256]{1,0:T(8,128)(2,1)S(1)}, bf16[32,16,128]{2,1,0:T(8,128)(2,1)S(1)}, f32[8,256]{1,0:T(8,128)S(1)}) custom-call(bf16[2,6,64,512]{3,2,1,0:T(8,128)(2,1)} %act.1, bf16[432,512]{1,0:T(8,128)(2,1)} %bitcast.7, bf16[64,3072]{1,0:T(8,128)(2,1)} %pw.1, f32[1,3072]{1,0:T(1,128)} %bitcast.9, f32[1,3072]{1,0:T(1,128)} %bitcast.10, ...), custom_call_target="tpu_custom_call" | custom-call | tf_op jit(solution)/shard_map/front/pallas_call | solution.py:420
  24.2 2.2 %back.1 = bf16[3,1536,256]{2,1,0:T(8,128)(2,1)} custom-call(bf16[1536,256]{1,0:T(8,128)(2,1)S(1)} %get-tuple-element.8.x_ref, bf16[32,16,128]{2,1,0:T(8,128)(2,1)S(1)} %get-tuple-element.9.m_ref, f32[8,256]{1,0:T(8,128)S(1)} %get-tuple-element.10.e_ref), custom_call_target="tpu_custom_call" | custom-call | tf_op jit(solution)/shard_map/back/pallas_call | solution.py:491

commit v3 on v2

--- a/solution.py
+++ b/solution.py
@@ -37,10 +37,10 @@
     act, cw, pw, pb, sh, sc, qw, qb, ng,
     x_out, m_out, e_out,
     act_v, cw_v, pw_v, pb_v, sh_v, sc_v, qw_v, qb_v, ng_v,
-    part, pair, share, got1, own, got2, m_all, prod,
+    part, pair, share, got1, own, own32, got2, m_all, prod,
     a_v, b_v, at_v, ab_v, bm_v, bt_v, bb_v,
     wst, x_all, r_all,
-    in_sem, act_sem, s0, g0, s1, g1, s3, g3, sx, gx, sh_sem, gh_sem,
+    in_sem, act_sem, go, s0, g0, s1, g1, sx, gx, sh_sem, gh_sem,
 ):
     wides, narrows, rows, width = sizes
     span = qw.shape[1]
@@ -56,10 +56,14 @@
     chip_y = me // DEPTHS
     chip_z = me % DEPTHS
     highs = chips // DEPTHS
-    each = share.shape[1]
+    half = share.shape[2]
+    each = 2 * half
+
+    def at(y, z, c):
+        return (y % highs * DEPTHS + z % DEPTHS) * CORES + c, n
 
     def core1(y, z):
-        return (y % highs * DEPTHS + z % DEPTHS) * CORES + CORES - 1, n
+        return at(y, z, CORES - 1)
 
     def landed(ref, sem):
         pltpu.make_async_copy(ref, ref, sem).wait()
@@ -82,33 +86,43 @@
     def greet(wide, narrow):
         pl.semaphore_signal(barrier, inc=1, device_id=(wide, narrow), device_id_type=MESH)
 
+    has_next = w < wides - 1
+    has_prev = w > 0
+    up = n > 0
+    down = n < narrows - 1
+    for i in range(1, highs):
+        greet(*core1(chip_y + i, chip_z))
+    for i in range(1, narrows):
+        greet(w + CORES - 1 - core, (n + i) % narrows)
+    greet(partner, n)
+
     @pl.when(sums)
     def _():
         for i in range(1, DEPTHS):
             greet(*core1(chip_y, chip_z + i))
-        for i in range(1, highs):
-            greet(*core1(chip_y + i, chip_z))
-
-    for i in range(1, narrows):
-        greet(w, (n + i) % narrows)
-    has_next = w < wides - 1
-    has_prev = w > 0
-    for there, dw in ((has_next, 1), (has_prev, -1)):
-        for dn in (-1, 0, 1):
-            inside = there
-            if dn == -1:
-                inside = jnp.logical_and(there, n > 0)
-            if dn == 1:
-                inside = jnp.logical_and(there, n < narrows - 1)
-
-            @pl.when(inside)
-            def _():
-                greet(w + dw, n + dn)
-
-    greet(partner, n)
-    sides = jnp.where(has_next, 1, 0) + jnp.where(has_prev, 1, 0)
-    across = 1 + jnp.where(n > 0, 1, 0) + jnp.where(n < narrows - 1, 1, 0)
-    expected = jnp.where(sums, DEPTHS + highs - 1, 1) + (narrows - 1) + sides * across
+
+        @pl.when(up)
+        def _():
+            greet(w, n - 1)
+
+        @pl.when(down)
+        def _():
+            greet(w, n + 1)
+
+    @pl.when(jnp.logical_and(jnp.logical_not(sums), has_prev))
+    def _():
+        greet(w - 1, n)
+
+        @pl.when(up)
+        def _():
+            greet(w - 1, n - 1)
+
+        @pl.when(down)
+        def _():
+            greet(w - 1, n + 1)
+
+    across = jnp.where(up, 1, 0) + jnp.where(down, 1, 0)
+    expected = CORES * (narrows - 1) + across + jnp.where(has_next, 1 + across, 0) + CORES * (highs - 1) + DEPTHS
 
     qw_v[:, span:, :] = jnp.zeros((3, qw_v.shape[1] - span, qw_v.shape[2]), BF16)
     for copy in loads[:5]:
@@ -134,11 +148,25 @@
         res = dot(hi, qw_v[j]) + dot(lo, qw_v[j])
         for head in range(2):
             part[15 * head + 5 * j : 15 * head + 5 * j + 5] = res[:, head * LANES : (head + 1) * LANES].reshape(5, 16, LANES)
+    def sent(src, dst, ssem, gsem, to):
+        return pltpu.make_async_remote_copy(
+            src_ref=src, dst_ref=dst, send_sem=ssem, recv_sem=gsem, device_id=to, device_id_type=MESH
+        )
+
+    pair_copy = sent(part, pair, s0.at[0], g0.at[0], (partner, n))
+
+    @pl.when(jnp.logical_not(sums))
+    def _():
+        pl.semaphore_wait(barrier, 1)
+        pair_copy.start()
+
     loads[5].wait()
     for k in range(pairs):
         landed(act_v.at[pl.ds(2 * k, 2)], act_sem.at[k])
+    for k in range(pairs):
         raw = act_v[2 * k : 2 * k + 2].reshape(256, act.shape[3]).astype(F32)
-        acted = (raw / (1.0 + jnp.exp(-raw))).astype(BF16)
+        less = 0.5 * raw
+        acted = (less + less * jnp.tanh(less)).astype(BF16)
         res = dot_t(cw_v[...], acted)
         prod[2 * k] = res[:, :LANES]
         prod[2 * k + 1] = res[:, LANES:]
@@ -172,21 +200,16 @@
     a_v[...] = here.reshape(rows + 2, 16, LANES)
     b_v[...] = ahead.reshape(rows + 2, 16, LANES)
 
-    pl.semaphore_wait(barrier, expected)
-
-    def sent(src, dst, ssem, gsem, to):
-        return pltpu.make_async_remote_copy(
-            src_ref=src, dst_ref=dst, send_sem=ssem, recv_sem=gsem, device_id=to, device_id_type=MESH
-        )
-
-    pair_copy = sent(part, pair, s0.at[0], g0.at[0], (partner, n))
+
+    @pl.when(sums)
+    def _():
+        pl.semaphore_wait(barrier, expected)
+        pl.semaphore_signal(go, inc=1, device_id=(partner, n), device_id_type=MESH)
 
     @pl.when(jnp.logical_not(sums))
     def _():
-        pair_copy.start()
-
-    up = n > 0
-    down = n < narrows - 1
+        pl.semaphore_wait(go, 1)
+
     edges = [
         (b_v.at[pl.ds(1, rows)], bm_v, has_next, has_prev, (w + 1, n)),
         (a_v.at[0], ab_v, up, down, (w, n - 1)),
@@ -212,7 +235,6 @@
     wst[64:] = lo
 
     row16 = lax.broadcasted_iota(jnp.int32, (16, LANES), 0)
-    last = sent(m_all, m_all, s3.at[0], g3.at[0], (partner, n))
 
     @pl.when(sums)
     def _():
@@ -222,23 +244,25 @@
             if tile % 5 == 4:
                 hi = total.astype(BF16).astype(F32)
                 total = jnp.where(row16 < 2, hi, pltpu.roll(total - hi, 2, 0))
-            share[tile // each, tile % each] = total.astype(BF16)
+            share[tile % each // half, tile // each, tile % half] = total.astype(BF16)
         for tile in range(30, highs * each):
-            share[tile // each, tile % each] = jnp.zeros((16, LANES), BF16)
-        for i in range(1, highs):
-            sent(
-                share.at[(chip_y + i) % highs], got1.at[i - 1], s1.at[0], g1.at[0], core1(chip_y + i, chip_z)
-            ).start()
-
-    @pl.when(sums)
-    def _():
-        landed(got1, g1.at[0])
-        total = share[chip_y].astype(F32)
-        for i in range(1, highs):
-            total = total + got1[i - 1].astype(F32)
-        own[...] = total.astype(BF16)
-        for i in range(1, DEPTHS):
-            sent(own, got2.at[i - 1], s1.at[1], g1.at[1], core1(chip_y, chip_z + i)).start()
+            share[tile % each // half, tile // each, tile % half] = jnp.zeros((16, LANES), BF16)
+        for p in range(2):
+            for i in range(1, highs):
+                to = (chip_y + i) % highs
+                sent(share.at[p, to], got1.at[p, i - 1], s1.at[p], g1.at[p], core1(to, chip_z)).start()
+
+    @pl.when(sums)
+    def _():
+        for p in range(2):
+            landed(got1.at[p], g1.at[p])
+            total = share[p, chip_y].astype(F32)
+            for i in range(1, highs):
+                total = total + got1[p, i - 1].astype(F32)
+            own32[p] = total
+            own[p] = total.astype(BF16)
+            for i in range(1, DEPTHS):
+                sent(own.at[p], got2.at[p, i - 1], s1.at[2 + p], g1.at[2 + p], core1(chip_y, chip_z + i)).start()
 
     for k, (src, dst, gives, gets, to) in enumerate(edges):
 
@@ -296,23 +320,25 @@
     for i in range(1, narrows):
         sent(r_all.at[n], r_all.at[n], sx.at[1], gx.at[1], (w, (n + i) % narrows)).start()
 
-    mine = m_all.at[pl.ds(each * chip_y, each)]
-
-    @pl.when(sums)
-    def _():
-        landed(got2, g1.at[1])
-        total = own[...].astype(F32)
-        for i in range(1, DEPTHS):
-            total = total + got2[i - 1].astype(F32)
-        for k in range(each):
-            plain = total[k]
-            both = plain + pltpu.roll(plain, 14, 0)
-            hi = both.astype(BF16).astype(F32)
-            both = jnp.where(row16 < 2, hi, pltpu.roll(both - hi, 2, 0))
-            tile = each * chip_y + k
-            m_all[tile] = jnp.where(tile % 5 == 4, both, plain).astype(BF16)
-        for i in range(1, highs):
-            sent(mine, mine, s1.at[2], g1.at[2], core1(chip_y + i, chip_z)).start()
+    @pl.when(sums)
+    def _():
+        for p in range(2):
+            landed(got2.at[p], g1.at[2 + p])
+            total = own32[p]
+            for i in range(1, DEPTHS):
+                total = total + got2[p, i - 1].astype(F32)
+            for k in range(half):
+                plain = total[k]
+                both = plain + pltpu.roll(plain, 14, 0)
+                hi = both.astype(BF16).astype(F32)
+                both = jnp.where(row16 < 2, hi, pltpu.roll(both - hi, 2, 0))
+                tile = each * chip_y + half * p + k
+                m_all[tile] = jnp.where(tile % 5 == 4, both, plain).astype(BF16)
+            mine = m_all.at[pl.ds(each * chip_y + half * p, half)]
+            for i in range(highs):
+                for c in range(CORES):
+                    if i > 0 or c < CORES - 1:
+                        sent(mine, mine, s1.at[4], g1.at[4], at(chip_y + i, chip_z, c)).start()
 
     loads[6].wait()
     loads[7].wait()
@@ -324,25 +350,26 @@
     turned = jnp.transpose(jnp.concatenate([flat, jnp.zeros((LANES - narrows * 8, LANES), F32)], axis=0))
     for src in range(narrows):
         theirs = x_all[src].astype(F32)
+        columns = [
+            jnp.broadcast_to(turned[:per, 8 * src + t : 8 * src + t + 1], (per, LANES)) for t in range(2)
+        ]
+        value = theirs * jnp.where(low, columns[0], columns[1])
+        hi = value.astype(BF16).astype(F32)
+        lo = value - hi
+        values = [jnp.where(low, hi, rolled(lo, 64)), jnp.where(low, rolled(hi, 64), lo)]
         for t in range(2):
-            column = turned[:per, 8 * src + t : 8 * src + t + 1]
-            value = theirs * column
-            hi = value.astype(BF16).astype(F32)
-            lo = value - hi
-            value = jnp.where(low, hi, rolled(lo, 64)) if t == 0 else jnp.where(low, rolled(hi, 64), lo)
-            hi = column.astype(BF16).astype(F32)
-            more = jnp.where(lane2 == 1, column - hi, jnp.where(lane2 < 3, hi, jnp.where(lane2 < 5, 1.0, 0.0)))
+            hi = columns[t].astype(BF16).astype(F32)
+            more = jnp.where(lane2 == 1, columns[t] - hi, jnp.where(lane2 < 3, hi, 1.0))
             place = pl.ds((t * narrows + src) * per, per)
-            x_out[place, :LANES] = value.astype(BF16)
+            x_out[place, :LANES] = values[t].astype(BF16)
             x_out[place, LANES:] = more.astype(BF16)
     @pl.when(sums)
     def _():
-        landed(m_all.at[pl.ds(0, each * (highs - 1))], g1.at[2])
-        last.start()
+        landed(m_all.at[pl.ds(0, each * (highs - 1))], g1.at[4])
 
     @pl.when(jnp.logical_not(sums))
     def _():
-        last.wait_recv()
+        landed(m_all, g1.at[4])
 
     m_out[...] = m_all[...]
     landed(x_all.at[pl.ds(0, narrows - 1)], sx.at[0])
@@ -350,10 +377,11 @@
 
     @pl.when(sums)
     def _():
-        landed(got1, s1.at[0])
-        landed(got2, s1.at[1])
-        landed(m_all.at[pl.ds(0, each * (highs - 1))], s1.at[2])
-        last.wait_send()
+        for p in range(2):
+            landed(got1.at[p], s1.at[p])
+            landed(got2.at[p], s1.at[2 + p])
+        landed(m_all, s1.at[4])
+        landed(m_all.at[pl.ds(0, each * (highs - 1))], s1.at[4])
 
     @pl.when(jnp.logical_not(sums))
     def _():
@@ -386,19 +414,19 @@
             rows = jnp.where(row16 == 4, constant - high, rows)
             mm[128:144, cols] = rows.astype(BF16)
     copies = []
-    for t in range(2):
+    half = tokens // 2
+    for part in range(4):
         for j in range(3):
-            product = dot(x_ref[t * tokens : (t + 1) * tokens], mm[:, 256 * j : 256 * j + 256])
+            place = pl.ds(part * half, half)
+            product = dot(x_ref[place], mm[:, 256 * j : 256 * j + 256])
             for hd in range(2):
                 cols = slice(LANES * hd, LANES * hd + LANES)
                 y = product[:, cols]
                 if j < 2:
                     mean = jnp.sum(y * y, axis=1, keepdims=True) * (1.0 / LANES)
                     y = y * lax.rsqrt(mean + 1e-06) * e_ref[3 + j : 4 + j, :LANES]
-                stage[3 * t + j, :, cols] = y.astype(BF16)
-            copy = pltpu.make_async_copy(
-                stage.at[3 * t + j], out.at[j, pl.ds(t * tokens, tokens)], sems.at[3 * t + j]
-            )
+                stage[j, place, cols] = y.astype(BF16)
+            copy = pltpu.make_async_copy(stage.at[j, place], out.at[j, place], sems.at[3 * part + j])
             copy.start()
             copies.append(copy)
     for copy in copies:
@@ -411,7 +439,7 @@
     taps = jnp.transpose(conv_weight, (0, 1, 2, 4, 3)).reshape(-1, channels)
     qkv = jnp.transpose(qkv_weight, (1, 0, 2))
     highs = wides // (CORES * DEPTHS)
-    each = -(-30 // highs)
+    half = -(-30 // (2 * highs))
     per = rows // 2 * cols // 2
     any_spec = pl.BlockSpec(memory_space=pltpu.HBM)
     vmem = pl.BlockSpec(memory_space=pltpu.VMEM)
@@ -421,7 +449,7 @@
         functools.partial(front, (wides, narrows, rows, width)),
         out_shape=[
             jax.ShapeDtypeStruct((2 * narrows * per, 2 * LANES), BF16),
-            jax.ShapeDtypeStruct((highs * each, 16, LANES), BF16),
+            jax.ShapeDtypeStruct((highs * 2 * half, 16, LANES), BF16),
             jax.ShapeDtypeStruct((8, 256), F32),
         ],
         in_specs=[any_spec] * 9,
@@ -438,11 +466,12 @@
             pltpu.VMEM(norm_gains.shape, F32),
             pltpu.VMEM((30, 16, LANES), F32),
             pltpu.VMEM((30, 16, LANES), F32),
-            pltpu.VMEM((highs, each, 16, LANES), BF16),
-            pltpu.VMEM((highs - 1, each, 16, LANES), BF16),
-            pltpu.VMEM((each, 16, LANES), BF16),
-            pltpu.VMEM((DEPTHS - 1, each, 16, LANES), BF16),
-            pltpu.VMEM((highs * each, 16, LANES), BF16),
+            pltpu.VMEM((2, highs, half, 16, LANES), BF16),
+            pltpu.VMEM((2, highs - 1, half, 16, LANES), BF16),
+            pltpu.VMEM((2, half, 16, LANES), BF16),
+            pltpu.VMEM((2, half, 16, LANES), F32),
+            pltpu.VMEM((2, DEPTHS - 1, half, 16, LANES), BF16),
+            pltpu.VMEM((highs * 2 * half, 16, LANES), BF16),
             pltpu.VMEM((rows, taps.shape[0], LANES), F32),
             pltpu.VMEM((rows + 2, 16, LANES), F32),
             pltpu.VMEM((rows + 2, 16, LANES), F32),
@@ -456,12 +485,11 @@
             pltpu.VMEM((narrows, 8, LANES), F32),
             dma((8,)),
             dma((rows // 2,)),
+            pltpu.SemaphoreType.REGULAR,
             dma((1,)),
             dma((1,)),
-            dma((3,)),
-            dma((3,)),
-            dma((1,)),
-            dma((1,)),
+            dma((5,)),
+            dma((5,)),
             dma((2,)),
             dma((2,)),
             dma((5,)),
@@ -495,8 +523,8 @@
         out_specs=any_spec,
         scratch_shapes=[
             pltpu.VMEM((2 * LANES, 768), BF16),
-            pltpu.VMEM((6, tokens, 256), BF16),
-            dma((6,)),
+            pltpu.VMEM((3, 2 * tokens, 256), BF16),
+            dma((12,)),
         ],
         compiler_params=pltpu.CompilerParams(vmem_limit_bytes=40 * 1024 * 1024),
         name="back",

time: 26.5 us -> 23.9 us (0.902)
  Pallas kernels: 26.4 us -> 23.8 us
    pallas_call x1, Pallas kernels: 24.2 us -> 21.6 us  [local(): pl.pallas_call(functools.partial(front, (wides, narrows, rows, width)), o...]
where the time goes in v3:
time: 23.9 us; the launch traced here: 23.8 us
  Pallas kernels  23.8 us (100%)
    pallas_call x1, Pallas kernels, local(): pl.pallas_call(functools.partial(front, (wides, narrows, rows, width)), o...  21.6 us
    pallas_call x1, Pallas kernels, local(): pl.pallas_call(back, out_shape=jax.ShapeDtypeStruct((3, 2 * tokens, 256),...  2.12 us

profile of v3, /device:TPU:1, one launch (start us, length us, event | category | flops | bytes accessed | tf_op | source)
XLA Modules:
  0.0 23.8 jit_solution(1607570184836888217)
XLA Ops:
  0.0 21.6 %front.1 = (bf16[1536,256]{1,0:T(8,128)(2,1)S(1)}, bf16[32,16,128]{2,1,0:T(8,128)(2,1)S(1)}, f32[8,256]{1,0:T(8,128)S(1)}) custom-call(bf16[2,6,64,512]{3,2,1,0:T(8,128)(2,1)} %act.1, bf16[432,512]{1,0:T(8,128)(2,1)} %bitcast.7, bf16[64,3072]{1,0:T(8,128)(2,1)} %pw.1, f32[1,3072]{1,0:T(1,128)} %bitcast.9, f32[1,3072]{1,0:T(1,128)} %bitcast.10, ...), custom_call_target="tpu_custom_call" | custom-call | tf_op jit(solution)/shard_map/front/pallas_call | solution.py:448
  21.6 2.1 %back.1 = bf16[3,1536,256]{2,1,0:T(8,128)(2,1)} custom-call(bf16[1536,256]{1,0:T(8,128)(2,1)S(1)} %get-tuple-element.8.x_ref, bf16[32,16,128]{2,1,0:T(8,128)(2,1)S(1)} %get-tuple-element.9.m_ref, f32[8,256]{1,0:T(8,128)S(1)} %get-tuple-element.10.e_ref), custom_call_target="tpu_custom_call" | custom-call | tf_op jit(solution)/shard_map/back/pallas_call | solution.py:519

commit v4 on v3

--- a/solution.py
+++ b/solution.py
@@ -92,8 +92,12 @@
     down = n < narrows - 1
     for i in range(1, highs):
         greet(*core1(chip_y + i, chip_z))
-    for i in range(1, narrows):
-        greet(w + CORES - 1 - core, (n + i) % narrows)
+    for other in range(narrows):
+
+        @pl.when(jnp.logical_or(n < other, n == other + 1))
+        def _():
+            greet(w + CORES - 1 - core, other)
+
     greet(partner, n)
 
     @pl.when(sums)
@@ -122,7 +126,7 @@
             greet(w - 1, n + 1)
 
     across = jnp.where(up, 1, 0) + jnp.where(down, 1, 0)
-    expected = CORES * (narrows - 1) + across + jnp.where(has_next, 1 + across, 0) + CORES * (highs - 1) + DEPTHS
+    expected = CORES * (n + jnp.where(down, 1, 0)) + across + jnp.where(has_next, 1 + across, 0) + CORES * (highs - 1) + DEPTHS
 
     qw_v[:, span:, :] = jnp.zeros((3, qw_v.shape[1] - span, qw_v.shape[2]), BF16)
     for copy in loads[:5]:
@@ -204,18 +208,23 @@
     @pl.when(sums)
     def _():
         pl.semaphore_wait(barrier, expected)
-        pl.semaphore_signal(go, inc=1, device_id=(partner, n), device_id_type=MESH)
+        pl.semaphore_signal(go.at[0], inc=1, device_id=(partner, n), device_id_type=MESH)
+        for other in range(narrows - 2):
+
+            @pl.when(other + 1 < n)
+            def _():
+                pl.semaphore_signal(go.at[1], inc=1, device_id=(w, other), device_id_type=MESH)
 
     @pl.when(jnp.logical_not(sums))
     def _():
-        pl.semaphore_wait(go, 1)
+        pl.semaphore_wait(go.at[0], 1)
 
     edges = [
+        (b_v.at[0], bb_v, jnp.logical_and(has_next, up), jnp.logical_and(has_prev, down), (w + 1, n - 1)),
+        (b_v.at[rows + 1], bt_v, jnp.logical_and(has_next, down), jnp.logical_and(has_prev, up), (w + 1, n + 1)),
         (b_v.at[pl.ds(1, rows)], bm_v, has_next, has_prev, (w + 1, n)),
         (a_v.at[0], ab_v, up, down, (w, n - 1)),
         (a_v.at[rows + 1], at_v, down, up, (w, n + 1)),
-        (b_v.at[0], bb_v, jnp.logical_and(has_next, up), jnp.logical_and(has_prev, down), (w + 1, n - 1)),
-        (b_v.at[rows + 1], bt_v, jnp.logical_and(has_next, down), jnp.logical_and(has_prev, up), (w + 1, n + 1)),
     ]
     edge_copies = []
     for k, (src, dst, gives, gets, to) in enumerate(edges):
@@ -252,8 +261,7 @@
                 to = (chip_y + i) % highs
                 sent(share.at[p, to], got1.at[p, i - 1], s1.at[p], g1.at[p], core1(to, chip_z)).start()
 
-    @pl.when(sums)
-    def _():
+    def first_sums():
         for p in range(2):
             landed(got1.at[p], g1.at[p])
             total = share[p, chip_y].astype(F32)
@@ -261,8 +269,16 @@
                 total = total + got1[p, i - 1].astype(F32)
             own32[p] = total
             own[p] = total.astype(BF16)
-            for i in range(1, DEPTHS):
-                sent(own.at[p], got2.at[p, i - 1], s1.at[2 + p], g1.at[2 + p], core1(chip_y, chip_z + i)).start()
+            for z in range(DEPTHS):
+
+                @pl.when(z != chip_z)
+                def _():
+                    slot = lax.rem(z - chip_z + DEPTHS, DEPTHS) - 1
+                    sent(own.at[p], got2.at[p, slot], s1.at[2 + p], g1.at[2 + p], core1(chip_y, z)).start()
+
+    @pl.when(jnp.logical_and(sums, chip_z > 0))
+    def _():
+        first_sums()
 
     for k, (src, dst, gives, gets, to) in enumerate(edges):
 
@@ -296,6 +312,20 @@
         patches.append(dot_t(pick, jnp.concatenate(blocks, axis=0)))
     x = jnp.concatenate(patches, axis=0)
     x_all[n] = x.astype(BF16)
+
+    @pl.when(sums)
+    def _():
+
+        @pl.when(n < narrows - 2)
+        def _():
+            pl.semaphore_wait(go.at[1], narrows - 2 - n)
+
+        pl.semaphore_signal(go.at[1], inc=1, device_id=(partner, n), device_id_type=MESH)
+
+    @pl.when(jnp.logical_not(sums))
+    def _():
+        pl.semaphore_wait(go.at[1], 1)
+
     for i in range(1, narrows):
         sent(x_all.at[n], x_all.at[n], sx.at[0], gx.at[0], (w, (n + i) % narrows)).start()
 
@@ -320,6 +350,10 @@
     for i in range(1, narrows):
         sent(r_all.at[n], r_all.at[n], sx.at[1], gx.at[1], (w, (n + i) % narrows)).start()
 
+    @pl.when(jnp.logical_and(sums, chip_z == 0))
+    def _():
+        first_sums()
+
     @pl.when(sums)
     def _():
         for p in range(2):
@@ -335,10 +369,13 @@
                 tile = each * chip_y + half * p + k
                 m_all[tile] = jnp.where(tile % 5 == 4, both, plain).astype(BF16)
             mine = m_all.at[pl.ds(each * chip_y + half * p, half)]
-            for i in range(highs):
-                for c in range(CORES):
-                    if i > 0 or c < CORES - 1:
-                        sent(mine, mine, s1.at[4], g1.at[4], at(chip_y + i, chip_z, c)).start()
+            for c in reversed(range(CORES)):
+                for y in range(highs):
+
+                    @pl.when(jnp.logical_or(y != chip_y, c != core))
+                    def _():
+                        sent(mine, mine, s1.at[4], g1.at[4], at(y, chip_z, c)).start()
+
 
     loads[6].wait()
     loads[7].wait()
@@ -356,7 +393,8 @@
         value = theirs * jnp.where(low, columns[0], columns[1])
         hi = value.astype(BF16).astype(F32)
         lo = value - hi
-        values = [jnp.where(low, hi, rolled(lo, 64)), jnp.where(low, rolled(hi, 64), lo)]
+        crossed = rolled(jnp.where(low, lo, hi), 64)
+        values = [jnp.where(low, hi, crossed), jnp.where(low, crossed, lo)]
         for t in range(2):
             hi = columns[t].astype(BF16).astype(F32)
             more = jnp.where(lane2 == 1, columns[t] - hi, jnp.where(lane2 < 3, hi, 1.0))
@@ -485,7 +523,7 @@
             pltpu.VMEM((narrows, 8, LANES), F32),
             dma((8,)),
             dma((rows // 2,)),
-            pltpu.SemaphoreType.REGULAR,
+            pltpu.SemaphoreType.REGULAR((2,)),
             dma((1,)),
             dma((1,)),
             dma((5,)),

time: 23.9 us -> 22.3 us (0.933)
  Pallas kernels: 23.8 us -> 22.2 us
    pallas_call x1, Pallas kernels: 21.6 us -> 20.1 us  [local(): pl.pallas_call(functools.partial(front, (wides, narrows, rows, width)), o...]
where the time goes in v4:
time: 22.3 us; the launch traced here: 22.2 us
  Pallas kernels  22.2 us (100%)
    pallas_call x1, Pallas kernels, local(): pl.pallas_call(functools.partial(front, (wides, narrows, rows, width)), o...  20.1 us
    pallas_call x1, Pallas kernels, local(): pl.pallas_call(back, out_shape=jax.ShapeDtypeStruct((3, 2 * tokens, 256),...  2.12 us

profile of v4, /device:TPU:1, one launch (start us, length us, event | category | flops | bytes accessed | tf_op | source)
XLA Modules:
  0.0 22.2 jit_solution(16295099609222891461)
XLA Ops:
  0.0 20.1 %front.1 = (bf16[1536,256]{1,0:T(8,128)(2,1)S(1)}, bf16[32,16,128]{2,1,0:T(8,128)(2,1)S(1)}, f32[8,256]{1,0:T(8,128)S(1)}) custom-call(bf16[2,6,64,512]{3,2,1,0:T(8,128)(2,1)} %act.1, bf16[432,512]{1,0:T(8,128)(2,1)} %bitcast.7, bf16[64,3072]{1,0:T(8,128)(2,1)} %pw.1, f32[1,3072]{1,0:T(1,128)} %bitcast.9, f32[1,3072]{1,0:T(1,128)} %bitcast.10, ...), custom_call_target="tpu_custom_call" | custom-call | tf_op jit(solution)/shard_map/front/pallas_call | solution.py:486
  20.1 2.1 %back.1 = bf16[3,1536,256]{2,1,0:T(8,128)(2,1)} custom-call(bf16[1536,256]{1,0:T(8,128)(2,1)S(1)} %get-tuple-element.8.x_ref, bf16[32,16,128]{2,1,0:T(8,128)(2,1)S(1)} %get-tuple-element.9.m_ref, f32[8,256]{1,0:T(8,128)S(1)} %get-tuple-element.10.e_ref), custom_call_target="tpu_custom_call" | custom-call | tf_op jit(solution)/shard_map/back/pallas_call | solution.py:557

commit v5 on v4

--- a/solution.py
+++ b/solution.py
@@ -1,4 +1,5 @@
 import functools
+import math
 
 import jax
 import jax.numpy as jnp
@@ -40,7 +41,7 @@
     part, pair, share, got1, own, own32, got2, m_all, prod,
     a_v, b_v, at_v, ab_v, bm_v, bt_v, bb_v,
     wst, x_all, r_all,
-    in_sem, act_sem, go, s0, g0, s1, g1, sx, gx, sh_sem, gh_sem,
+    in_sem, go, out_sem, g0, g1, gx, gh_sem,
 ):
     wides, narrows, rows, width = sizes
     span = qw.shape[1]
@@ -68,18 +69,24 @@
     def landed(ref, sem):
         pltpu.make_async_copy(ref, ref, sem).wait()
 
-    loads = []
-    for k, (src, dst) in enumerate(
-        [(pw, pw_v), (sc, sc_v), (sh, sh_v), (pb, pb_v), (qw, qw_v.at[:, pl.ds(0, span), :]), (cw, cw_v), (qb, qb_v), (ng, ng_v)]
-    ):
-        copy = pltpu.make_async_copy(src, dst, in_sem.at[k])
-        copy.start()
-        loads.append(copy)
-    for k in range(pairs):
-        for t in range(2):
-            pltpu.make_async_copy(
-                act.at[t, pl.ds(2 * k, 2)], act_v.at[pl.ds(2 * k, 2), t], act_sem.at[k]
-            ).start()
+    def lines(*refs):
+        return sum(math.prod(ref.shape) * ref.dtype.itemsize for ref in refs) // (4 * LANES)
+
+    def landed_lines(count, sem):
+        planes = 4 if count % 4 == 0 and count // 4 <= prod.shape[1] else rows
+        landed(prod.at[pl.ds(0, planes), pl.ds(0, count // planes)], sem)
+
+    qw_part = qw_v.at[:, pl.ds(0, span), :]
+    small = [(sc, sc_v), (sh, sh_v), (pb, pb_v), (qb, qb_v), (ng, ng_v)]
+    pltpu.make_async_copy(pw, pw_v, in_sem.at[0]).start()
+    for k, (src, dst) in enumerate(small[:3]):
+        pltpu.make_async_copy(src, dst, in_sem.at[2 + k]).start()
+    pltpu.make_async_copy(qw, qw_part, in_sem.at[0]).start()
+    pltpu.make_async_copy(cw, cw_v, in_sem.at[1]).start()
+    for t in range(2):
+        pltpu.make_async_copy(act.at[t], act_v.at[:, t], in_sem.at[1]).start()
+    for k, (src, dst) in enumerate(small[3:]):
+        pltpu.make_async_copy(src, dst, in_sem.at[5 + k]).start()
 
     barrier = pltpu.get_barrier_semaphore()
 
@@ -129,8 +136,9 @@
     expected = CORES * (n + jnp.where(down, 1, 0)) + across + jnp.where(has_next, 1 + across, 0) + CORES * (highs - 1) + DEPTHS
 
     qw_v[:, span:, :] = jnp.zeros((3, qw_v.shape[1] - span, qw_v.shape[2]), BF16)
-    for copy in loads[:5]:
-        copy.wait()
+    landed_lines(lines(pw_v, qw_part), in_sem.at[0])
+    for k in range(3):
+        landed(small[k][1], in_sem.at[2 + k])
     weight = pw_v[...].astype(F32)
     means = jnp.sum(weight, axis=1, keepdims=True) * (1.0 / width)
     bias_mean = jnp.sum(pb_v[...], axis=1, keepdims=True) * (1.0 / width)
@@ -157,16 +165,14 @@
             src_ref=src, dst_ref=dst, send_sem=ssem, recv_sem=gsem, device_id=to, device_id_type=MESH
         )
 
-    pair_copy = sent(part, pair, s0.at[0], g0.at[0], (partner, n))
+    pair_copy = sent(part, pair, out_sem.at[0], g0.at[0], (partner, n))
 
     @pl.when(jnp.logical_not(sums))
     def _():
         pl.semaphore_wait(barrier, 1)
         pair_copy.start()
 
-    loads[5].wait()
-    for k in range(pairs):
-        landed(act_v.at[pl.ds(2 * k, 2)], act_sem.at[k])
+    landed_lines(lines(cw_v, act_v), in_sem.at[1])
     for k in range(pairs):
         raw = act_v[2 * k : 2 * k + 2].reshape(256, act.shape[3]).astype(F32)
         less = 0.5 * raw
@@ -228,7 +234,7 @@
     ]
     edge_copies = []
     for k, (src, dst, gives, gets, to) in enumerate(edges):
-        copy = sent(src, dst, sh_sem.at[k], gh_sem.at[k], to)
+        copy = sent(src, dst, out_sem.at[0], gh_sem.at[0], to)
         edge_copies.append(copy)
 
         @pl.when(gives)
@@ -238,10 +244,6 @@
         @pl.when(jnp.logical_not(gets))
         def _():
             dst[...] = jnp.zeros(dst.shape, F32)
-
-    hi, lo = halves(weight - means)
-    wst[:64] = hi
-    wst[64:] = lo
 
     row16 = lax.broadcasted_iota(jnp.int32, (16, LANES), 0)
 
@@ -259,7 +261,11 @@
         for p in range(2):
             for i in range(1, highs):
                 to = (chip_y + i) % highs
-                sent(share.at[p, to], got1.at[p, i - 1], s1.at[p], g1.at[p], core1(to, chip_z)).start()
+                sent(share.at[p, to], got1.at[p, i - 1], out_sem.at[0], g1.at[p], core1(to, chip_z)).start()
+
+    hi, lo = halves(weight - means)
+    wst[:64] = hi
+    wst[64:] = lo
 
     def first_sums():
         for p in range(2):
@@ -274,17 +280,24 @@
                 @pl.when(z != chip_z)
                 def _():
                     slot = lax.rem(z - chip_z + DEPTHS, DEPTHS) - 1
-                    sent(own.at[p], got2.at[p, slot], s1.at[2 + p], g1.at[2 + p], core1(chip_y, z)).start()
+                    sent(own.at[p], got2.at[p, slot], out_sem.at[0], g1.at[2 + p], core1(chip_y, z)).start()
 
     @pl.when(jnp.logical_and(sums, chip_z > 0))
     def _():
         first_sums()
 
-    for k, (src, dst, gives, gets, to) in enumerate(edges):
-
-        @pl.when(gets)
-        def _():
-            edge_copies[k].wait_recv()
+    edge = lines(a_v.at[0])
+    main = lines(bm_v)
+    beside = jnp.where(up, 1, 0) + jnp.where(down, 1, 0)
+    for sides in (1, 2):
+
+        @pl.when(jnp.logical_and(beside == sides, has_prev))
+        def _():
+            landed_lines(main + 2 * sides * edge, gh_sem.at[0])
+
+        @pl.when(jnp.logical_and(beside == sides, jnp.logical_not(has_prev)))
+        def _():
+            landed_lines(sides * edge, gh_sem.at[0])
 
     lane1 = lax.broadcasted_iota(jnp.int32, (16, LANES), 1)
     pick = jnp.where(
@@ -327,7 +340,7 @@
         pl.semaphore_wait(go.at[1], 1)
 
     for i in range(1, narrows):
-        sent(x_all.at[n], x_all.at[n], sx.at[0], gx.at[0], (w, (n + i) % narrows)).start()
+        sent(x_all.at[n], x_all.at[n], out_sem.at[0], gx.at[0], (w, (n + i) % narrows)).start()
 
     per = x.shape[0]
     other = rolled(x, 64)
@@ -344,11 +357,15 @@
     spread = jnp.sum(squares, axis=1, keepdims=True) * (1.0 / width)
     factor = lax.rsqrt(spread + 1e-06)
     lane2 = lax.broadcasted_iota(jnp.int32, (per, LANES), 1)
-    placed = jnp.where(lane2 == 0, factor[:per], jnp.where(lane2 == 1, factor[per:], 0.0))
+    chosen = jnp.where(lane2 < 3, factor[:per], factor[per:])
+    hi = chosen.astype(BF16).astype(F32)
+    mid = (chosen - hi).astype(BF16).astype(F32)
+    chosen = jnp.where(lane2 % 3 == 0, hi, jnp.where(lane2 % 3 == 1, mid, chosen - hi - mid))
+    placed = jnp.where(lane2 < 6, chosen, jnp.where(lane2 == 6, 1.0, 0.0))
     placed = jnp.concatenate([placed, jnp.zeros((LANES - per, LANES), F32)], axis=0)
-    r_all[n] = jnp.transpose(placed)[:8]
+    r_all[n] = jnp.transpose(placed)[:16].astype(BF16)
     for i in range(1, narrows):
-        sent(r_all.at[n], r_all.at[n], sx.at[1], gx.at[1], (w, (n + i) % narrows)).start()
+        sent(r_all.at[n], r_all.at[n], out_sem.at[0], gx.at[1], (w, (n + i) % narrows)).start()
 
     @pl.when(jnp.logical_and(sums, chip_z == 0))
     def _():
@@ -374,33 +391,36 @@
 
                     @pl.when(jnp.logical_or(y != chip_y, c != core))
                     def _():
-                        sent(mine, mine, s1.at[4], g1.at[4], at(y, chip_z, c)).start()
-
-
-    loads[6].wait()
-    loads[7].wait()
+                        sent(mine, mine, out_sem.at[0], g1.at[4], at(y, chip_z, c)).start()
+
+
+    landed(qb_v, in_sem.at[5])
+    landed(ng_v, in_sem.at[6])
     e_out[0:3] = qb_v[...]
     e_out[3:5, :LANES] = ng_v[...]
     landed(x_all.at[pl.ds(0, narrows - 1)], gx.at[0])
     landed(r_all.at[pl.ds(0, narrows - 1)], gx.at[1])
-    flat = r_all[...].reshape(narrows * 8, LANES)
-    turned = jnp.transpose(jnp.concatenate([flat, jnp.zeros((LANES - narrows * 8, LANES), F32)], axis=0))
+    term = lax.broadcasted_iota(jnp.int32, (16, 3 * LANES), 0)
+    place = lax.broadcasted_iota(jnp.int32, (16, 3 * LANES), 1)
+    spot = place % LANES
+    frame = jnp.where(place < LANES, spot // 64, place // LANES - 1)
+    wanted = jnp.where(place < LANES, 0, jnp.where(spot < 3, 1, jnp.where(spot < 5, 2, 3)))
+    taken = (wanted == 0) & (term // 3 == frame)
+    taken = taken | ((wanted == 1) & (term == 3 * frame + spot % 2)) | ((wanted == 2) & (term == 6))
+    spread_out = jnp.where(taken, 1.0, 0.0).astype(BF16)
     for src in range(narrows):
-        theirs = x_all[src].astype(F32)
-        columns = [
-            jnp.broadcast_to(turned[:per, 8 * src + t : 8 * src + t + 1], (per, LANES)) for t in range(2)
-        ]
-        value = theirs * jnp.where(low, columns[0], columns[1])
+        table = lax.dot_general(
+            r_all[src], spread_out, (((0,), (0,)), ((), ())), preferred_element_type=F32
+        )[:per]
+        value = x_all[src].astype(F32) * table[:, :LANES]
         hi = value.astype(BF16).astype(F32)
         lo = value - hi
         crossed = rolled(jnp.where(low, lo, hi), 64)
         values = [jnp.where(low, hi, crossed), jnp.where(low, crossed, lo)]
         for t in range(2):
-            hi = columns[t].astype(BF16).astype(F32)
-            more = jnp.where(lane2 == 1, columns[t] - hi, jnp.where(lane2 < 3, hi, 1.0))
             place = pl.ds((t * narrows + src) * per, per)
             x_out[place, :LANES] = values[t].astype(BF16)
-            x_out[place, LANES:] = more.astype(BF16)
+            x_out[place, LANES:] = table[:, LANES * (t + 1) : LANES * (t + 2)].astype(BF16)
     @pl.when(sums)
     def _():
         landed(m_all.at[pl.ds(0, each * (highs - 1))], g1.at[4])
@@ -410,26 +430,18 @@
         landed(m_all, g1.at[4])
 
     m_out[...] = m_all[...]
-    landed(x_all.at[pl.ds(0, narrows - 1)], sx.at[0])
-    landed(r_all.at[pl.ds(0, narrows - 1)], sx.at[1])
-
-    @pl.when(sums)
-    def _():
-        for p in range(2):
-            landed(got1.at[p], s1.at[p])
-            landed(got2.at[p], s1.at[2 + p])
-        landed(m_all, s1.at[4])
-        landed(m_all.at[pl.ds(0, each * (highs - 1))], s1.at[4])
-
-    @pl.when(jnp.logical_not(sums))
-    def _():
-        pair_copy.wait_send()
-
-    for k, (src, dst, gives, gets, to) in enumerate(edges):
-
-        @pl.when(gives)
-        def _():
-            edge_copies[k].wait_send()
+    always = (narrows - 1) * (lines(x_all) + lines(r_all)) // narrows
+    spread_lines = (CORES * highs - 1) * lines(m_all) // highs
+    for sides in (1, 2):
+        for follows in (False, True):
+            for adds in (False, True):
+                gone = always + sides * edge + (main + sides * edge if follows else 0)
+                gone += lines(got1, got2) + spread_lines if adds else lines(part)
+                here_so = jnp.logical_and(beside == sides, has_next == follows)
+
+                @pl.when(jnp.logical_and(here_so, sums == adds))
+                def _():
+                    landed_lines(gone, out_sem.at[0])
 
 
 def back(x_ref, m_ref, e_ref, out, mm, stage, sems):
@@ -451,7 +463,6 @@
             rows = jnp.where(row16 == 3, high, rows)
             rows = jnp.where(row16 == 4, constant - high, rows)
             mm[128:144, cols] = rows.astype(BF16)
-    copies = []
     half = tokens // 2
     for part in range(4):
         for j in range(3):
@@ -464,11 +475,9 @@
                     mean = jnp.sum(y * y, axis=1, keepdims=True) * (1.0 / LANES)
                     y = y * lax.rsqrt(mean + 1e-06) * e_ref[3 + j : 4 + j, :LANES]
                 stage[j, place, cols] = y.astype(BF16)
-            copy = pltpu.make_async_copy(stage.at[j, place], out.at[j, place], sems.at[3 * part + j])
+            copy = pltpu.make_async_copy(stage.at[j, place], out.at[j, place], sems.at[0])
             copy.start()
-            copies.append(copy)
-    for copy in copies:
-        copy.wait()
+    pltpu.make_async_copy(stage, out, sems.at[0]).wait()
 
 
 def local(wides, narrows, activations, conv_weight, patch_weight, patch_bias, shift, scale, qkv_weight, qkv_bias, norm_gains):
@@ -520,18 +529,14 @@
             edge,
             pltpu.VMEM((LANES, width), BF16),
             pltpu.VMEM((narrows, per, LANES), BF16),
-            pltpu.VMEM((narrows, 8, LANES), F32),
-            dma((8,)),
-            dma((rows // 2,)),
+            pltpu.VMEM((narrows, 16, LANES), BF16),
+            dma((7,)),
             pltpu.SemaphoreType.REGULAR((2,)),
             dma((1,)),
             dma((1,)),
             dma((5,)),
-            dma((5,)),
             dma((2,)),
-            dma((2,)),
-            dma((5,)),
-            dma((5,)),
+            dma((1,)),
         ],
         compiler_params=pltpu.CompilerParams(
             collective_id=0, has_side_effects=True, vmem_limit_bytes=40 * 1024 * 1024
@@ -562,7 +567,7 @@
         scratch_shapes=[
             pltpu.VMEM((2 * LANES, 768), BF16),
             pltpu.VMEM((3, 2 * tokens, 256), BF16),
-            dma((12,)),
+            dma((1,)),
         ],
         compiler_params=pltpu.CompilerParams(vmem_limit_bytes=40 * 1024 * 1024),
         name="back",

time: 22.3 us -> 21.9 us (0.982)
  Pallas kernels: 22.2 us -> 21.8 us
    pallas_call x1, Pallas kernels: 20.1 us -> 19.8 us  [local(): pl.pallas_call(functools.partial(front, (wides, narrows, rows, width)), o...]
where the time goes in v5:
time: 21.9 us; the launch traced here: 21.8 us
  Pallas kernels  21.8 us (100%)
    pallas_call x1, Pallas kernels, local(): pl.pallas_call(functools.partial(front, (wides, narrows, rows, width)), o...  19.8 us
    pallas_call x1, Pallas kernels, local(): pl.pallas_call(back, out_shape=jax.ShapeDtypeStruct((3, 2 * tokens, 256),...  2.02 us

profile of v5, /device:TPU:1, one launch (start us, length us, event | category | flops | bytes accessed | tf_op | source)
XLA Modules:
  0.0 21.8 jit_solution(3468634080561833234)
XLA Ops:
  0.0 19.8 %front.1 = (bf16[1536,256]{1,0:T(8,128)(2,1)S(1)}, bf16[32,16,128]{2,1,0:T(8,128)(2,1)S(1)}, f32[8,256]{1,0:T(8,128)S(1)}) custom-call(bf16[2,6,64,512]{3,2,1,0:T(8,128)(2,1)} %act.1, bf16[432,512]{1,0:T(8,128)(2,1)} %bitcast.7, bf16[64,3072]{1,0:T(8,128)(2,1)} %pw.1, f32[1,3072]{1,0:T(1,128)} %bitcast.9, f32[1,3072]{1,0:T(1,128)} %bitcast.10, ...), custom_call_target="tpu_custom_call" | custom-call | tf_op jit(solution)/shard_map/front/pallas_call | solution.py:495
  19.8 2.0 %back.1 = bf16[3,1536,256]{2,1,0:T(8,128)(2,1)} custom-call(bf16[1536,256]{1,0:T(8,128)(2,1)S(1)} %get-tuple-element.8.x_ref, bf16[32,16,128]{2,1,0:T(8,128)(2,1)S(1)} %get-tuple-element.9.m_ref, f32[8,256]{1,0:T(8,128)S(1)} %get-tuple-element.10.e_ref), custom_call_target="tpu_custom_call" | custom-call | tf_op jit(solution)/shard_map/back/pallas_call | solution.py:562

commit v6 on v5

--- a/solution.py
+++ b/solution.py
@@ -339,8 +339,13 @@
     def _():
         pl.semaphore_wait(go.at[1], 1)
 
-    for i in range(1, narrows):
-        sent(x_all.at[n], x_all.at[n], out_sem.at[0], gx.at[0], (w, (n + i) % narrows)).start()
+    far_first = [(2, 1), (1, 1), (3, 1), (2, 0), (1, 0), (3, 0), (0, 1)]
+    others = [((n // 2 + dx) % (narrows // 2)) * 2 + (n + dl) % 2 for dx, dl in far_first]
+    def send_patches(targets):
+        for other in targets:
+            sent(x_all.at[n], x_all.at[n], out_sem.at[0], gx.at[0], (w, other)).start()
+
+    send_patches(others[:3])
 
     per = x.shape[0]
     other = rolled(x, 64)
@@ -364,12 +369,21 @@
     placed = jnp.where(lane2 < 6, chosen, jnp.where(lane2 == 6, 1.0, 0.0))
     placed = jnp.concatenate([placed, jnp.zeros((LANES - per, LANES), F32)], axis=0)
     r_all[n] = jnp.transpose(placed)[:16].astype(BF16)
-    for i in range(1, narrows):
-        sent(r_all.at[n], r_all.at[n], out_sem.at[0], gx.at[1], (w, (n + i) % narrows)).start()
+    for other in others:
+        sent(r_all.at[n], r_all.at[n], out_sem.at[0], gx.at[1], (w, other)).start()
+    send_patches(others[3:])
 
     @pl.when(jnp.logical_and(sums, chip_z == 0))
     def _():
         first_sums()
+
+    def spread(p, c):
+        mine = m_all.at[pl.ds(each * chip_y + half * p, half)]
+        for y in range(highs):
+
+            @pl.when(jnp.logical_or(y != chip_y, c != core))
+            def _():
+                sent(mine, mine, out_sem.at[0], g1.at[4], at(y, chip_z, c)).start()
 
     @pl.when(sums)
     def _():
@@ -385,14 +399,9 @@
                 both = jnp.where(row16 < 2, hi, pltpu.roll(both - hi, 2, 0))
                 tile = each * chip_y + half * p + k
                 m_all[tile] = jnp.where(tile % 5 == 4, both, plain).astype(BF16)
-            mine = m_all.at[pl.ds(each * chip_y + half * p, half)]
-            for c in reversed(range(CORES)):
-                for y in range(highs):
-
-                    @pl.when(jnp.logical_or(y != chip_y, c != core))
-                    def _():
-                        sent(mine, mine, out_sem.at[0], g1.at[4], at(y, chip_z, c)).start()
-
+            spread(p, CORES - 1)
+        for p in range(2):
+            spread(p, 0)
 
     landed(qb_v, in_sem.at[5])
     landed(ng_v, in_sem.at[6])

time: 21.9 us -> 21.6 us (0.986)
  Pallas kernels: 21.8 us -> 21.4 us
    pallas_call x1, Pallas kernels: 19.8 us -> 19.4 us  [local(): pl.pallas_call(functools.partial(front, (wides, narrows, rows, width)), o...]
where the time goes in v6:
time: 21.6 us; the launch traced here: 21.5 us
  Pallas kernels  21.4 us (99%)
    pallas_call x1, Pallas kernels, local(): pl.pallas_call(functools.partial(front, (wides, narrows, rows, width)), o...  19.4 us
    pallas_call x1, Pallas kernels, local(): pl.pallas_call(back, out_shape=jax.ShapeDtypeStruct((3, 2 * tokens, 256),...  2.02 us

profile of v6, /device:TPU:1, one launch (start us, length us, event | category | flops | bytes accessed | tf_op | source)
XLA Modules:
  0.0 21.5 jit_solution(15769388585239336967)
XLA Ops:
  0.0 19.4 %front.1 = (bf16[1536,256]{1,0:T(8,128)(2,1)S(1)}, bf16[32,16,128]{2,1,0:T(8,128)(2,1)S(1)}, f32[8,256]{1,0:T(8,128)S(1)}) custom-call(bf16[2,6,64,512]{3,2,1,0:T(8,128)(2,1)} %act.1, bf16[432,512]{1,0:T(8,128)(2,1)} %bitcast.7, bf16[64,3072]{1,0:T(8,128)(2,1)} %pw.1, f32[1,3072]{1,0:T(1,128)} %bitcast.9, f32[1,3072]{1,0:T(1,128)} %bitcast.10, ...), custom_call_target="tpu_custom_call" | custom-call | tf_op jit(solution)/shard_map/front/pallas_call | solution.py:504
  19.4 2.0 %back.1 = bf16[3,1536,256]{2,1,0:T(8,128)(2,1)} custom-call(bf16[1536,256]{1,0:T(8,128)(2,1)S(1)} %get-tuple-element.8.x_ref, bf16[32,16,128]{2,1,0:T(8,128)(2,1)S(1)} %get-tuple-element.9.m_ref, f32[8,256]{1,0:T(8,128)S(1)} %get-tuple-element.10.e_ref), custom_call_target="tpu_custom_call" | custom-call | tf_op jit(solution)/shard_map/back/pallas_call | solution.py:571

commit v7 on v6

--- a/solution.py
+++ b/solution.py
@@ -345,7 +345,7 @@
         for other in targets:
             sent(x_all.at[n], x_all.at[n], out_sem.at[0], gx.at[0], (w, other)).start()
 
-    send_patches(others[:3])
+    send_patches(others[:4])
 
     per = x.shape[0]
     other = rolled(x, 64)
@@ -371,7 +371,7 @@
     r_all[n] = jnp.transpose(placed)[:16].astype(BF16)
     for other in others:
         sent(r_all.at[n], r_all.at[n], out_sem.at[0], gx.at[1], (w, other)).start()
-    send_patches(others[3:])
+    send_patches(others[4:])
 
     @pl.when(jnp.logical_and(sums, chip_z == 0))
     def _():

time: 21.6 us -> 21.6 us (level)
  no operation moved by 1% of the time
where the time goes in v7:
time: 21.6 us; the launch traced here: 21.5 us
  Pallas kernels  21.4 us (99%)
    pallas_call x1, Pallas kernels, local(): pl.pallas_call(functools.partial(front, (wides, narrows, rows, width)), o...  19.4 us
    pallas_call x1, Pallas kernels, local(): pl.pallas_call(back, out_shape=jax.ShapeDtypeStruct((3, 2 * tokens, 256),...  2.02 us

profile of v7, /device:TPU:1, one launch (start us, length us, event | category | flops | bytes accessed | tf_op | source)
XLA Modules:
  0.0 21.5 jit_solution(17438532819468200923)
XLA Ops:
  0.0 19.4 %front.1 = (bf16[1536,256]{1,0:T(8,128)(2,1)S(1)}, bf16[32,16,128]{2,1,0:T(8,128)(2,1)S(1)}, f32[8,256]{1,0:T(8,128)S(1)}) custom-call(bf16[2,6,64,512]{3,2,1,0:T(8,128)(2,1)} %act.1, bf16[432,512]{1,0:T(8,128)(2,1)} %bitcast.7, bf16[64,3072]{1,0:T(8,128)(2,1)} %pw.1, f32[1,3072]{1,0:T(1,128)} %bitcast.9, f32[1,3072]{1,0:T(1,128)} %bitcast.10, ...), custom_call_target="tpu_custom_call" | custom-call | tf_op jit(solution)/shard_map/front/pallas_call | solution.py:504
  19.4 2.0 %back.1 = bf16[3,1536,256]{2,1,0:T(8,128)(2,1)} custom-call(bf16[1536,256]{1,0:T(8,128)(2,1)S(1)} %get-tuple-element.8.x_ref, bf16[32,16,128]{2,1,0:T(8,128)(2,1)S(1)} %get-tuple-element.9.m_ref, f32[8,256]{1,0:T(8,128)S(1)} %get-tuple-element.10.e_ref), custom_call_target="tpu_custom_call" | custom-call | tf_op jit(solution)/shard_map/back/pallas_call | solution.py:571

commit v8 on v7

--- a/solution.py
+++ b/solution.py
@@ -267,6 +267,12 @@
     wst[:64] = hi
     wst[64:] = lo
 
+    def send_own(p, z):
+        @pl.when(z != chip_z)
+        def _():
+            slot = lax.rem(z - chip_z + DEPTHS, DEPTHS) - 1
+            sent(own.at[p], got2.at[p, slot], out_sem.at[0], g1.at[2 + p], core1(chip_y, z)).start()
+
     def first_sums():
         for p in range(2):
             landed(got1.at[p], g1.at[p])
@@ -275,12 +281,10 @@
                 total = total + got1[p, i - 1].astype(F32)
             own32[p] = total
             own[p] = total.astype(BF16)
-            for z in range(DEPTHS):
-
-                @pl.when(z != chip_z)
-                def _():
-                    slot = lax.rem(z - chip_z + DEPTHS, DEPTHS) - 1
-                    sent(own.at[p], got2.at[p, slot], out_sem.at[0], g1.at[2 + p], core1(chip_y, z)).start()
+            send_own(p, 0)
+        for z in range(1, DEPTHS):
+            for p in range(2):
+                send_own(p, z)
 
     @pl.when(jnp.logical_and(sums, chip_z > 0))
     def _():

time: 21.6 us -> 21.6 us (level)
  no operation moved by 1% of the time
where the time goes in v8:
time: 21.6 us; the launch traced here: 21.5 us
  Pallas kernels  21.5 us (100%)
    pallas_call x1, Pallas kernels, local(): pl.pallas_call(functools.partial(front, (wides, narrows, rows, width)), o...  19.5 us
    pallas_call x1, Pallas kernels, local(): pl.pallas_call(back, out_shape=jax.ShapeDtypeStruct((3, 2 * tokens, 256),...  2.01 us

profile of v8, /device:TPU:1, one launch (start us, length us, event | category | flops | bytes accessed | tf_op | source)
XLA Modules:
  0.0 21.5 jit_solution(9569321461109527073)
XLA Ops:
  0.0 19.5 %front.1 = (bf16[1536,256]{1,0:T(8,128)(2,1)S(1)}, bf16[32,16,128]{2,1,0:T(8,128)(2,1)S(1)}, f32[8,256]{1,0:T(8,128)S(1)}) custom-call(bf16[2,6,64,512]{3,2,1,0:T(8,128)(2,1)} %act.1, bf16[432,512]{1,0:T(8,128)(2,1)} %bitcast.7, bf16[64,3072]{1,0:T(8,128)(2,1)} %pw.1, f32[1,3072]{1,0:T(1,128)} %bitcast.9, f32[1,3072]{1,0:T(1,128)} %bitcast.10, ...), custom_call_target="tpu_custom_call" | custom-call | tf_op jit(solution)/shard_map/front/pallas_call | solution.py:508
  19.5 2.0 %back.1 = bf16[3,1536,256]{2,1,0:T(8,128)(2,1)} custom-call(bf16[1536,256]{1,0:T(8,128)(2,1)S(1)} %get-tuple-element.8.x_ref, bf16[32,16,128]{2,1,0:T(8,128)(2,1)S(1)} %get-tuple-element.9.m_ref, f32[8,256]{1,0:T(8,128)S(1)} %get-tuple-element.10.e_ref), custom_call_target="tpu_custom_call" | custom-call | tf_op jit(solution)/shard_map/back/pallas_call | solution.py:575
